TPU v7x, 256 devices: a whole 4x4x8 slice. The times are simulated.
256 devices in a mesh: pool: 32 (over x, z_hi, y), tp: 8 (over z_lo, core).
Axes of the slice: x: 4, y: 4, z: 8 (z_hi: 2, z_lo: 4; z = z_hi * 4 + z_lo), core: 2. Of those that a mesh axis runs over, the one named last changes fastest.
Arguments:
- queries: bfloat16 [16384, 4096], P('pool', 'tp'), may hold values from -400 to 400
- new_keys: bfloat16 [16384, 1024], P('pool', 'tp'), may hold values from -400 to 400
- new_values: bfloat16 [16384, 1024], P('pool', 'tp'), may hold values from -6 to 6
- kv_pool: bfloat16 [6144, 2, 64, 1024], P('pool', None, None, 'tp'), may hold values from -6 to 6
- out_weight: bfloat16 [4096, 4096], P('tp'), may hold values from -0.09375 to 0.09375
- prefix_len: int32 [32], P('pool'), may hold values from 1 to 8192
- new_count: int32 [32], P('pool'), may hold values from 1 to 512
- hit_holder: int32 [32, 128], P('pool'), may hold values from 0 to 31, as said below
- hit_block: int32 [32, 128], P('pool'), may hold values from 0 to 191
- decode_owner: int32 [32, 32], P('pool'), may hold values from 0 to 31, as said below
Outputs:
- projected: bfloat16 [16384, 4096], P(('pool', 'tp'))
- decode_pages: bfloat16 [32, 32, 1, 2, 16, 1024], P('pool', None, None, None, None, 'tp')
Inputs may be any that keep to these rules, and one draw needn't show every extreme that they name: `hit_holder`: each request's 128 entries name every pool index exactly 4 times. `decode_owner`: each request's 32 entries name every pool index exactly 1 times.
All inputs are finite; a program needn't handle non-finite values.
Results may differ from a plain program's by a relative error of at most 0.017.
Values may be sent and summed in bfloat16 or wider, within the bound.
No kernel may reach another device: no remote copies, remote signals or barrier semaphores. Data moves between devices by JAX's collectives and lax.ppermute only.
A program may use at most 128 MiB of HBM per device.

v0:
```python
import jax
import jax.numpy as jnp
from jax import lax
from jax.sharding import PartitionSpec as P

HD = 128
PG = 16


def pick_rows(items, picks):
    return jax.vmap(lambda single, chosen: single[chosen])(items, picks)


def push_pages(new_keys, new_values, live, decode_owner):
    req_dev, page_count = decode_owner.shape
    n_pool = lax.axis_size("pool")
    per_owner = page_count // n_pool
    width = new_keys.shape[1]
    new_tok = new_keys.shape[0] // req_dev
    keep = live.astype(jnp.bfloat16)[:, :, None]
    key_rows = new_keys.reshape(req_dev, new_tok, width) * keep
    value_rows = new_values.reshape(req_dev, new_tok, width) * keep
    both = jnp.stack([key_rows, value_rows], axis=1).reshape(req_dev, 2, page_count, PG, width)
    both = jnp.transpose(both, (0, 2, 1, 3, 4))
    order = jnp.argsort(decode_owner, axis=1, stable=True)
    ordered = pick_rows(both, order).reshape(req_dev, n_pool, per_owner, 2, PG, width)
    outgoing = jnp.transpose(ordered, (1, 0, 2, 3, 4, 5))
    arrived = lax.all_to_all(outgoing, "pool", split_axis=0, concat_axis=0, tiled=True)
    return arrived.reshape(1, n_pool * req_dev, per_owner, 2, PG, width)


def attend(query_rows, keys, values, prefix_ok, new_tok, group):
    rows_all = query_rows.shape[0]
    block_rows = min(512, rows_all)
    scale = HD ** (-0.5)

    def one_block(index):
        query_block = lax.dynamic_slice_in_dim(query_rows, index * block_rows, block_rows, 0)
        scores = (
            lax.dot_general(
                query_block, keys, (((1,), (1,)), ((), ())), preferred_element_type=jnp.float32
            )
            * scale
        )
        token = (index * block_rows + jnp.arange(block_rows, dtype=jnp.int32)) // group
        causal = jnp.arange(new_tok, dtype=jnp.int32)[None, :] <= token[:, None]
        allowed = jnp.concatenate(
            [jnp.broadcast_to(prefix_ok[None, :], (block_rows, prefix_ok.shape[0])), causal], axis=1
        )
        scores = jnp.where(allowed, scores, -jnp.inf)
        peak = jnp.max(scores, axis=1, keepdims=True)
        weights = jnp.exp(scores - peak)
        total = jnp.sum(weights, axis=1, keepdims=True)
        mixed = jnp.dot(weights.astype(jnp.bfloat16), values, preferred_element_type=jnp.float32)
        return (mixed / total).astype(jnp.bfloat16)

    blocks_out = lax.map(one_block, jnp.arange(rows_all // block_rows, dtype=jnp.int32))
    return blocks_out.reshape(rows_all, HD)


def local(
    queries,
    new_keys,
    new_values,
    kv_pool,
    out_weight,
    prefix_len,
    new_count,
    hit_holder,
    hit_block,
    decode_owner,
):
    req_dev, slots = hit_holder.shape
    n_pool = lax.axis_size("pool")
    per_holder = slots // n_pool
    new_tok = queries.shape[0] // req_dev
    width = new_keys.shape[1]
    kv_local = width // HD
    group = queries.shape[1] // width
    block_len = kv_pool.shape[2]
    live = jnp.arange(new_tok, dtype=jnp.int32)[None, :] < new_count[:, None]
    order = jnp.argsort(hit_holder, axis=1, stable=True)
    sorted_ids = pick_rows(hit_block, order).reshape(req_dev, n_pool, per_holder)
    ids_in = lax.all_to_all(sorted_ids, "pool", split_axis=1, concat_axis=1, tiled=True)
    outgoing = kv_pool[ids_in]
    arrived = lax.all_to_all(outgoing, "pool", split_axis=1, concat_axis=1, tiled=True)
    prefix_pos = (
        order[:, :, None] * block_len + jnp.arange(block_len, dtype=jnp.int32)[None, None, :]
    ).reshape(req_dev, slots * block_len)
    prefix_ok = prefix_pos < prefix_len[:, None]
    prefix_keys = arrived[0, :, :, 0].reshape(slots * block_len, width)
    prefix_values = arrived[0, :, :, 1].reshape(slots * block_len, width)
    query_req = queries.reshape(new_tok, kv_local, group, HD)
    keys = jnp.concatenate([prefix_keys, new_keys], axis=0)
    values = jnp.concatenate([prefix_values, new_values], axis=0)
    query_rows = query_req[:, 0].reshape(new_tok * group, HD)
    result = attend(query_rows, keys, values, prefix_ok[0], new_tok, group)
    heads = [result.reshape(new_tok, group, HD)]
    joined = jnp.stack(heads, axis=1).reshape(new_tok, kv_local * group * HD)
    outputs = joined * live[0].astype(jnp.bfloat16)[:, None]
    summed = lax.psum_scatter(
        jnp.dot(outputs, out_weight, preferred_element_type=jnp.float32).astype(jnp.bfloat16),
        "tp",
        scatter_dimension=0,
        tiled=True,
    )
    pages = push_pages(new_keys, new_values, live, decode_owner)
    return (summed, pages)


def solution(mesh):
    in_specs = (
        P("pool", "tp"),
        P("pool", "tp"),
        P("pool", "tp"),
        P("pool", None, None, "tp"),
        P("tp", None),
        P("pool"),
        P("pool"),
        P("pool", None),
        P("pool", None),
        P("pool", None),
    )
    out_specs = (P(("pool", "tp"), None), P("pool", None, None, None, None, "tp"))
    return jax.shard_map(local, mesh=mesh, in_specs=in_specs, out_specs=out_specs, check_vma=False)
```

profile of v0, /device:TPU:28, one launch (start us, length us, event | category | flops | bytes accessed | tf_op | source)
XLA Modules:
  0.0 355.3 jit_solution(2023579496472783878)
XLA Ops:
  7.2 0.5 iota.47
  7.7 0.2 sort.37.cloned.1.call-update
  7.9 5.2 %sort.37.cloned.1.call-done = (s32[1,128]{1,0:T(1,128)}, s32[1,128]{1,0:T(1,128)}) async-done(((s32[1,128]{1,0:T(1,128)}, s32[1,128]{1,0:T(1,128)}), (s32[1,128]{1,0:T(1,128)}, s32[1,128]{1,0:T(1,128)})) %sort.37.cloned.1.call-update) | async-done | bytes 1040 | tf_op jit(solution)/shard_map/jit(argsort)/sort | solution.py:82
  13.1 0.7 multiply_bitcast_fusion
  13.8 1.2 gather_fusion.1
  15.0 0.1 reshape.114
  15.1 22.3 %all_to_all.15 = s32[1,32,4]{2,0,1:T(1,128)S(1)} all-to-all(s32[1,32,4]{2,0,1:T(1,128)S(1)} %bitcast.53), channel_id=1, replica_groups=mesh['pool'=32,'tp'=8] {'pool'}, dimensions={1} | all-to-all | bytes 1024 | tf_op jit(solution)/shard_map/all_to_all | solution.py:84
  37.4 0.1 fusion.27
  37.5 0.1 reshape.118
  37.6 5.8 %gather_fusion = bf16[128,2,64,128]{3,2,1,0:T(8,128)(2,1)} fusion(bf16[192,2,64,128]{3,2,1,0:T(8,128)(2,1)} %param.15, s32[1024]{0:T(1024)S(1)} %pad_clamp_fusion), kind=kCustom, calls=%fused_computation | custom fusion | bytes 8389120 | tf_op jit(solution)/shard_map/gather | solution.py:85
  43.4 5.5 %copy.21 = bf16[1,32,4,2,64,128]{5,4,2,3,0,1:T(8,128)(2,1)} copy(bf16[1,32,4,2,64,128]{5,4,3,2,1,0:T(8,128)(2,1)} %bitcast.46) | data formatting | bytes 8388608 | tf_op jit(solution)/shard_map/gather | solution.py:85
  48.9 8.5 %all-to-all-start.1 = ((bf16[1,32,4,2,64,128]{5,4,2,3,0,1:T(8,128)(2,1)}), bf16[1,32,4,2,64,128]{5,4,2,3,0,1:T(8,128)(2,1)}, u32[]{:S(2)}, u32[]{:S(2)}) async-start(bf16[1,32,4,2,64,128]{5,4,2,3,0,1:T(8,128)(2,1)} %copy.21), calls=%async_computation.1 | async-start | bytes 8388608 | tf_op jit(solution)/shard_map/all_to_all | solution.py:86
  57.5 0.3 reshape_squeeze_reshape.3
  58.5 92.4 %all-to-all-done.1 = bf16[1,32,4,2,64,128]{5,4,2,3,0,1:T(8,128)(2,1)} async-done(((bf16[1,32,4,2,64,128]{5,4,2,3,0,1:T(8,128)(2,1)}), bf16[1,32,4,2,64,128]{5,4,2,3,0,1:T(8,128)(2,1)}, u32[]{:S(2)}, u32[]{:S(2)}) %all-to-all-start.1) | async-done | bytes 4194336 | tf_op jit(solution)/shard_map/all_to_all | solution.py:86
  150.9 3.2 fusion.31
  154.1 5.7 %pad_maximum_fusion = (bf16[8704,128]{1,0:T(8,128)(2,1)}, bf16[8704,128]{1,0:T(8,128)(2,1)S(1)}) fusion(bf16[512,128]{1,0:T(8,128)(2,1)S(1)} %copy-done.1, bf16[8192,128]{1,0:T(8,128)(2,1)S(1)} %bitcast.48, bf16[512,128]{1,0:T(8,128)(2,1)S(1)} %copy-done.2, bf16[8192,128]{1,0:T(8,128)(2,1)S(1)} %bitcast.47), kind=kLoop, calls=%fused_computation.28 | loop fusion | flops 8912896 | bytes 8912896 | tf_op jit(solution)/shard_map/concatenate | solution.py:94
  159.9 118.8 %while.13 = (s32[]{:T(128)}, bf16[4,512,128]{2,1,0:T(8,128)(2,1)}, s32[4]{0:T(128)S(1)}, bf16[2048,128]{1,0:T(8,128)(2,1)S(1)}, bf16[8704,128]{1,0:T(8,128)(2,1)...) while((s32[]{:T(128)}, bf16[4,512,128]{2,1,0:T(8,128)(2,1)}, ...), condition=%wide.region_4.5_spmd.clone, body=%wide.region_1.4_spmd.clone.sunk | while | flops 2317769728 | bytes 59032260 | solution.py:57
  159.9 0.7 dynamic_slice.22
  161.2 0.2 iota_compare_fusion.3
  161.5 0.1 add.169
  161.5 0.1 add.170
  161.7 0.1 add.172
  161.8 0.8 compare_reduce_fusion.2
  162.5 9.2 %fusion.44 = (f32[512]{0:T(512)S(1)}, f32[512,8704]{1,0:T(8,128)}) fusion(bf16[8704,128]{1,0:T(8,128)(2,1)} %get-tuple-element.230, bf16[2048,128]{1,0:T(8,128)(2,1)S(1)} %get-tuple-element.229, s32[]{:T(128)S(6)} %select_n.54, pred[512,512]{1,0:T(32,128)(4,1)S(1)} %iota_compare_fusion.3, pred[8704]{0:T(1024)(128)(4,1)S(1)} %pad.2.clone.2), kind=kOutput, calls=%fused_computation.49.clone.1 | convolution fusion | flops 1158675968 | bytes 20458500 | tf_op jit(solution)/shard_map/while/body/eval_jaxpr/dot_general | solution.py:40
  171.7 8.5 %fusion.45 = f32[512]{0:T(512)S(1)} fusion(f32[512,8704]{1,0:T(8,128)} %get-tuple-element.198, f32[512]{0:T(512)S(1)} %get-tuple-element.199), kind=kLoop, calls=%fused_computation.6.clone.1 | loop fusion | flops 8912384 | bytes 17829888 | tf_op jit(solution)/shard_map/while/body/eval_jaxpr/reduce_sum | solution.py:53
  180.2 9.3 %fusion.46 = bf16[4,512,128]{2,1,0:T(8,128)(2,1)} fusion(bf16[4,512,128]{2,1,0:T(8,128)(2,1)} %get-tuple-element.214, s32[]{:T(128)} %get-tuple-element.213, bf16[8704,128]{1,0:T(8,128)(2,1)S(1)} %get-tuple-element.231, f32[512,8704]{1,0:T(8,128)} %get-tuple-element.198, f32[512]{0:T(512)S(1)} %get-tuple-element.199, f32[512]{0:T(512)S(1)} %fusion.45), kind=kOutput, calls=%fused_computation.13.clone.1 | convolution fusion | flops 1149894656 | bytes 20189696 | tf_op jit(solution)/shard_map/while/body/eval_jaxpr/dot_general | solution.py:54
  189.6 0.7 dynamic_slice.22
  190.9 0.2 iota_compare_fusion.3
  191.2 0.1 add.169
  191.2 0.1 add.170
  191.4 0.1 add.172
  191.5 0.8 compare_reduce_fusion.2
  192.2 9.2 %fusion.44 = (f32[512]{0:T(512)S(1)}, f32[512,8704]{1,0:T(8,128)}) fusion(bf16[8704,128]{1,0:T(8,128)(2,1)} %get-tuple-element.230, bf16[2048,128]{1,0:T(8,128)(2,1)S(1)} %get-tuple-element.229, s32[]{:T(128)S(6)} %select_n.54, pred[512,512]{1,0:T(32,128)(4,1)S(1)} %iota_compare_fusion.3, pred[8704]{0:T(1024)(128)(4,1)S(1)} %pad.2.clone.2), kind=kOutput, calls=%fused_computation.49.clone.1 | convolution fusion | flops 1158675968 | bytes 20458500 | tf_op jit(solution)/shard_map/while/body/eval_jaxpr/dot_general | solution.py:40
  201.4 8.5 %fusion.45 = f32[512]{0:T(512)S(1)} fusion(f32[512,8704]{1,0:T(8,128)} %get-tuple-element.198, f32[512]{0:T(512)S(1)} %get-tuple-element.199), kind=kLoop, calls=%fused_computation.6.clone.1 | loop fusion | flops 8912384 | bytes 17829888 | tf_op jit(solution)/shard_map/while/body/eval_jaxpr/reduce_sum | solution.py:53
  209.9 9.3 %fusion.46 = bf16[4,512,128]{2,1,0:T(8,128)(2,1)} fusion(bf16[4,512,128]{2,1,0:T(8,128)(2,1)} %get-tuple-element.214, s32[]{:T(128)} %get-tuple-element.213, bf16[8704,128]{1,0:T(8,128)(2,1)S(1)} %get-tuple-element.231, f32[512,8704]{1,0:T(8,128)} %get-tuple-element.198, f32[512]{0:T(512)S(1)} %get-tuple-element.199, f32[512]{0:T(512)S(1)} %fusion.45), kind=kOutput, calls=%fused_computation.13.clone.1 | convolution fusion | flops 1149894656 | bytes 20189696 | tf_op jit(solution)/shard_map/while/body/eval_jaxpr/dot_general | solution.py:54
  219.3 0.7 dynamic_slice.22
  220.6 0.2 iota_compare_fusion.3
  220.9 0.1 add.169
  220.9 0.1 add.170
  221.1 0.1 add.172
  221.2 0.8 compare_reduce_fusion.2
  221.9 9.2 %fusion.44 = (f32[512]{0:T(512)S(1)}, f32[512,8704]{1,0:T(8,128)}) fusion(bf16[8704,128]{1,0:T(8,128)(2,1)} %get-tuple-element.230, bf16[2048,128]{1,0:T(8,128)(2,1)S(1)} %get-tuple-element.229, s32[]{:T(128)S(6)} %select_n.54, pred[512,512]{1,0:T(32,128)(4,1)S(1)} %iota_compare_fusion.3, pred[8704]{0:T(1024)(128)(4,1)S(1)} %pad.2.clone.2), kind=kOutput, calls=%fused_computation.49.clone.1 | convolution fusion | flops 1158675968 | bytes 20458500 | tf_op jit(solution)/shard_map/while/body/eval_jaxpr/dot_general | solution.py:40
  231.1 8.5 %fusion.45 = f32[512]{0:T(512)S(1)} fusion(f32[512,8704]{1,0:T(8,128)} %get-tuple-element.198, f32[512]{0:T(512)S(1)} %get-tuple-element.199), kind=kLoop, calls=%fused_computation.6.clone.1 | loop fusion | flops 8912384 | bytes 17829888 | tf_op jit(solution)/shard_map/while/body/eval_jaxpr/reduce_sum | solution.py:53
  239.6 9.3 %fusion.46 = bf16[4,512,128]{2,1,0:T(8,128)(2,1)} fusion(bf16[4,512,128]{2,1,0:T(8,128)(2,1)} %get-tuple-element.214, s32[]{:T(128)} %get-tuple-element.213, bf16[8704,128]{1,0:T(8,128)(2,1)S(1)} %get-tuple-element.231, f32[512,8704]{1,0:T(8,128)} %get-tuple-element.198, f32[512]{0:T(512)S(1)} %get-tuple-element.199, f32[512]{0:T(512)S(1)} %fusion.45), kind=kOutput, calls=%fused_computation.13.clone.1 | convolution fusion | flops 1149894656 | bytes 20189696 | tf_op jit(solution)/shard_map/while/body/eval_jaxpr/dot_general | solution.py:54
  249.0 0.7 dynamic_slice.22
  250.3 0.2 iota_compare_fusion.3
  250.6 0.1 add.169
  250.6 0.1 add.170
  250.8 0.1 add.172
  250.9 0.8 compare_reduce_fusion.2
  251.6 9.2 %fusion.44 = (f32[512]{0:T(512)S(1)}, f32[512,8704]{1,0:T(8,128)}) fusion(bf16[8704,128]{1,0:T(8,128)(2,1)} %get-tuple-element.230, bf16[2048,128]{1,0:T(8,128)(2,1)S(1)} %get-tuple-element.229, s32[]{:T(128)S(6)} %select_n.54, pred[512,512]{1,0:T(32,128)(4,1)S(1)} %iota_compare_fusion.3, pred[8704]{0:T(1024)(128)(4,1)S(1)} %pad.2.clone.2), kind=kOutput, calls=%fused_computation.49.clone.1 | convolution fusion | flops 1158675968 | bytes 20458500 | tf_op jit(solution)/shard_map/while/body/eval_jaxpr/dot_general | solution.py:40
  260.8 8.5 %fusion.45 = f32[512]{0:T(512)S(1)} fusion(f32[512,8704]{1,0:T(8,128)} %get-tuple-element.198, f32[512]{0:T(512)S(1)} %get-tuple-element.199), kind=kLoop, calls=%fused_computation.6.clone.1 | loop fusion | flops 8912384 | bytes 17829888 | tf_op jit(solution)/shard_map/while/body/eval_jaxpr/reduce_sum | solution.py:53
  269.3 9.3 %fusion.46 = bf16[4,512,128]{2,1,0:T(8,128)(2,1)} fusion(bf16[4,512,128]{2,1,0:T(8,128)(2,1)} %get-tuple-element.214, s32[]{:T(128)} %get-tuple-element.213, bf16[8704,128]{1,0:T(8,128)(2,1)S(1)} %get-tuple-element.231, f32[512,8704]{1,0:T(8,128)} %get-tuple-element.198, f32[512]{0:T(512)S(1)} %get-tuple-element.199, f32[512]{0:T(512)S(1)} %fusion.45), kind=kOutput, calls=%fused_computation.13.clone.1 | convolution fusion | flops 1149894656 | bytes 20189696 | tf_op jit(solution)/shard_map/while/body/eval_jaxpr/dot_general | solution.py:54
  278.7 1.4 reshape_stack_reshape_reshape.3
  280.0 6.5 %convolution_convert_fusion = bf16[512,4096]{1,0:T(8,128)(2,1)} fusion(bf16[512,4096]{1,0:T(8,128)(2,1)} %param.16, bf16[512,512]{1,0:T(8,128)(2,1)S(1)} %reshape_stack_reshape_reshape.3, bf16[512]{0:T(512)(128)(2,1)S(1)} %fusion.28), kind=kOutput, calls=%fused_computation.27 | convolution fusion | flops 2149842944 | bytes 8913920 | tf_op jit(solution)/shard_map/dot_general | solution.py:102
  286.6 0.6 copy-done.4
  287.2 0.1 copy.22
  287.3 0.8 sort.35
  288.1 0.1 fusion.26
  288.2 0.1 broadcast_multiply_fusion.1
  288.4 0.6 gather_fusion.2
  289.0 24.6 %all_to_all.16 = bf16[32,1,1,2,16,128]{5,4,3,2,1,0:T(8,128)(2,1)S(1)} all-to-all(bf16[32,1,1,2,16,128]{5,4,3,2,1,0:T(8,128)(2,1)S(1)} %bitcast.50), channel_id=1, replica_groups=mesh['pool'=32,'tp'=8] {'pool'}, dimensions={0} | all-to-all | bytes 524288 | tf_op jit(solution)/shard_map/all_to_all | solution.py:28
  313.7 34.1 %reduce-scatter.2.cloned.1.call-done = bf16[64,4096]{1,0:T(8,128)(2,1)} async-done(((bf16[512,4096]{1,0:T(8,128)(2,1)}), bf16[64,4096]{1,0:T(8,128)(2,1)}) %reduce-scatter.2.cloned.1.call-update) | async-done | bytes 524304 | tf_op jit(solution)/shard_map/reduce_scatter | solution.py:101
  347.8 0.7 copy.35
  (34 shorter events, 0.3 us)
Async XLA Ops:
  7.2 6.6 %copy-start = (s32[1,128]{1,0:T(1,128)S(1)}, s32[1,128]{1,0:T(1,128)}, u32[]{:S(2)}) copy-start(s32[1,128]{1,0:T(1,128)} %param.20) | copy-start | bytes 1540
  7.2 5.9 %sort.37.cloned.1.call-start = ((), (), s32[]{:S(2)}) async-start(), calls=%async_computation.5 | async-start | bytes 3104 | tf_op jit(solution)/shard_map/jit(argsort)/sort | solution.py:82
  48.9 8.6 %copy-start.3 = (bf16[512,512]{1,0:T(8,128)(2,1)S(1)}, bf16[512,512]{1,0:T(8,128)(2,1)}, u32[]{:S(2)}) copy-start(bf16[512,512]{1,0:T(8,128)(2,1)} %param.12) | copy-start | bytes 1572868
  48.9 102.0 %all-to-all-start.1 = ((bf16[1,32,4,2,64,128]{5,4,2,3,0,1:T(8,128)(2,1)}), bf16[1,32,4,2,64,128]{5,4,2,3,0,1:T(8,128)(2,1)}, u32[]{:S(2)}, u32[]{:S(2)}) async-start(bf16[1,32,4,2,64,128]{5,4,2,3,0,1:T(8,128)(2,1)} %copy.21), calls=%async_computation.1 | async-start | bytes 8388608 | tf_op jit(solution)/shard_map/all_to_all | solution.py:86
  57.5 290.3 %reduce-scatter.2.cloned.1.call-start = ((), (), s32[]{:S(2)}) async-start(), calls=%async_computation.4 | async-start | bytes 4718592 | tf_op jit(solution)/shard_map/reduce_scatter | solution.py:101
  58.5 95.6 %copy-start.1 = (bf16[512,128]{1,0:T(8,128)(2,1)S(1)}, bf16[512,128]{1,0:T(8,128)(2,1)}, u32[]{:S(2)}) copy-start(bf16[512,128]{1,0:T(8,128)(2,1)} %param.13) | copy-start | bytes 393220
  58.5 95.6 %copy-start.2 = (bf16[512,128]{1,0:T(8,128)(2,1)S(1)}, bf16[512,128]{1,0:T(8,128)(2,1)}, u32[]{:S(2)}) copy-start(bf16[512,128]{1,0:T(8,128)(2,1)} %param.14) | copy-start | bytes 393220
  286.5 0.7 copy-start.4
Sparse Core Ops, SparseCore 0:
  10.8 2.0 sort.39.cloned.1.call-done
  286.7 61.0 reduce-scatter.1
  (1 shorter events, 0.0 us)
where the time goes:
time: 357 us; the launch traced here: 355 us
  waiting for transfers between devices  126 us (35%)
  matrix products  80.4 us (23%)
  blocking collectives  46.9 us (13%)
  other arithmetic  45.7 us (13%)
  local copies, waits for them, and re-layouts  29.5 us (8%)
  between operations  14.8 us (4%)
  starting transfers between devices  8.56 us (2%)
    all_to_all x1, waiting for transfers between devices, local(): lax.all_to_all(outgoing, 'pool', split_axis=1, concat_axis=1, tiled=True)  92.4 us
    dot_general x4, matrix products, one_block(): jnp.dot(weights.astype(jnp.bfloat16), values, preferred_element_type=jnp....  37.3 us
    dot_general x4, matrix products, one_block(): lax.dot_general(query_block, keys, (((1,), (1,)), ((), ())), preferred_el...  36.6 us
    reduce_sum x4, other arithmetic, one_block(): total = jnp.sum(weights, axis=1, keepdims=True)  34.2 us
    reduce_scatter x1, waiting for transfers between devices, local(): lax.psum_scatter(jnp.dot(outputs, out_weight, preferred_element_type=jnp....  34.1 us
    all_to_all x1, blocking collectives, push_pages(): lax.all_to_all(outgoing, 'pool', split_axis=0, concat_axis=0, tiled=True)  24.6 us
    all_to_all x1, blocking collectives, local(): lax.all_to_all(sorted_ids, 'pool', split_axis=1, concat_axis=1, tiled=True)  22.3 us
    gather x2, local copies, waits for them, and re-layouts, local(): outgoing = kv_pool[ids_in]  11.4 us
  transfers between devices with their start and end apart: 2, of which 2 were waited for; matrix products, arithmetic and copies ran while one was open for 1% of the time, Pallas kernels for 0%

commit v1 on v0

v1 whole, which is shorter than its diff:
```python
import functools
import jax
import jax.numpy as jnp
from jax import lax
from jax.experimental import pallas as pl
from jax.experimental.pallas import tpu as pltpu

HD = 128
NEG = -1e30
VMEM_LIMIT = 50 * 1024 * 1024
LOG2E = 1.4426950408889634


def tile_lanes(x, times):
    return x if times == 1 else jnp.concatenate([x] * times, axis=1)


def softmax_step(q, k, v, ok, m_prev, l_prev, acc_prev):
    c = HD ** (-0.5) * LOG2E
    width = k.shape[0] // HD
    s = lax.dot_general(q, k, (((1,), (1,)), ((), ())), preferred_element_type=jnp.float32)
    if ok is not None:
        s = jnp.where(ok, s, NEG)
    m_next = jnp.maximum(m_prev, jnp.max(s, axis=1, keepdims=True))
    p = jnp.exp2((s - tile_lanes(m_next, width)) * c)
    if ok is not None:
        p = jnp.where(ok, p, 0.0)
    alpha = jnp.exp2((m_prev - m_next) * c)
    part = p[:, :HD]
    for i in range(1, width):
        part = part + p[:, i * HD : (i + 1) * HD]
    mixed = jnp.dot(p.astype(jnp.bfloat16), v, preferred_element_type=jnp.float32)
    return m_next, alpha * l_prev + part, alpha * acc_prev + mixed


def prefix_pass(tab, q_ref, kv_hbm, kbuf, vbuf, acc, m_s, l_s, order, sems, ck, tb):
    holders, _, _, bl, _ = kv_hbm.shape
    n = order.shape[0]
    each = n // holders
    heads, tokens, _ = acc.shape
    per = ck // bl
    length, count = tab[n], tab[n + 1]

    def classify(i, carry):
        full, partial = carry
        left = length - tab[i] * bl

        @pl.when(left >= bl)
        def _():
            order[full] = i

        return (
            full + (left >= bl).astype(jnp.int32),
            jnp.where((left > 0) & (left < bl), i, partial),
        )

    full, partial = lax.fori_loop(0, n, classify, (jnp.int32(0), jnp.int32(-1)))
    has = (partial >= 0).astype(jnp.int32)

    @pl.when(partial >= 0)
    def _():
        order[full] = partial

    blocks = full + has
    rest = jnp.where(has > 0, length - tab[jnp.maximum(partial, 0)] * bl, 0)
    keys = full * bl + rest
    chunks = (blocks + per - 1) // per

    def load(i, carry):
        src = jnp.where(i < blocks, order[jnp.minimum(i, blocks - 1)], 0)
        at = pl.ds(pl.multiple_of(i * bl, bl), bl)
        pltpu.make_async_copy(kv_hbm.at[src // each, src % each, 0], kbuf.at[at], sems.at[0, i // per]).start()
        pltpu.make_async_copy(kv_hbm.at[src // each, src % each, 1], vbuf.at[at], sems.at[1, i // per]).start()
        return carry

    lax.fori_loop(0, chunks * per, load, 0)
    live_blocks = (count + tb - 1) // tb

    def one_chunk(ci, carry):
        at = pl.ds(pl.multiple_of(ci * ck, ck), ck)
        pltpu.make_async_copy(kbuf.at[at], kbuf.at[at], sems.at[0, ci]).wait()
        pltpu.make_async_copy(vbuf.at[at], vbuf.at[at], sems.at[1, ci]).wait()

        def rows(t, masked):
            k, v = kbuf[at], vbuf[at]
            ok = None
            if masked:
                ok = lax.broadcasted_iota(jnp.int32, (tb, ck), 1) < keys - ci * ck
            tok = pl.ds(pl.multiple_of(t * tb, tb), tb)
            for g in range(heads):
                m, l, a = softmax_step(
                    q_ref[tok, g * HD : (g + 1) * HD], k, v, ok,
                    m_s[g, tok], l_s[g, tok], acc[g, tok],
                )
                m_s[g, tok], l_s[g, tok], acc[g, tok] = m, l, a

        whole = keys >= (ci + 1) * ck

        @pl.when(whole)
        def _():
            lax.fori_loop(0, live_blocks, lambda t, x: (rows(t, False), x)[1], 0)

        @pl.when(jnp.logical_not(whole))
        def _():
            lax.fori_loop(0, live_blocks, lambda t, x: (rows(t, True), x)[1], 0)

        return carry

    lax.fori_loop(0, chunks, one_chunk, 0)


def reset(acc, m_s, l_s):
    acc[...] = jnp.zeros_like(acc)
    l_s[...] = jnp.zeros_like(l_s)
    m_s[...] = jnp.full_like(m_s, NEG)


def partner_kernel(tab, q_ref, kv_hbm, o_ref, st_ref, kbuf, vbuf, acc, m_s, l_s, order, sems, *, ck, tb):
    reset(acc, m_s, l_s)
    prefix_pass(tab, q_ref, kv_hbm, kbuf, vbuf, acc, m_s, l_s, order, sems, ck, tb)
    heads = acc.shape[0]
    lane = lax.broadcasted_iota(jnp.int32, m_s.shape[1:], 1)
    st = jnp.zeros(m_s.shape[1:], jnp.float32)
    for g in range(heads):
        total = jnp.sum(l_s[g], axis=1, keepdims=True)
        safe = jnp.where(total > 0, total, 1.0)
        o_ref[:, g * HD : (g + 1) * HD] = (acc[g] / safe).astype(o_ref.dtype)
        st = jnp.where(lane == g, m_s[g], st)
        st = jnp.where(lane == heads + g, total, st)
    st_ref[...] = st.T[: 2 * heads]


def scratch(n, heads, tokens, bl, ck):
    keys = n * bl
    return [
        pltpu.VMEM((keys, HD), jnp.bfloat16),
        pltpu.VMEM((keys, HD), jnp.bfloat16),
        pltpu.VMEM((heads, tokens, HD), jnp.float32),
        pltpu.VMEM((heads, tokens, HD), jnp.float32),
        pltpu.VMEM((heads, tokens, HD), jnp.float32),
        pltpu.SMEM((n,), jnp.int32),
        pltpu.SemaphoreType.DMA((2, keys // ck)),
    ]


VM = pl.BlockSpec(memory_space=pltpu.VMEM)
SM = pl.BlockSpec(memory_space=pltpu.SMEM)
ANY = pl.BlockSpec(memory_space=pl.ANY)


def partner_attention(tab, q, kv, ck=512, tb=256):
    n, bl = tab.shape[0] - 2, kv.shape[3]
    tokens, width = q.shape
    heads = width // HD
    return pl.pallas_call(
        functools.partial(partner_kernel, ck=ck, tb=tb),
        out_shape=[
            jax.ShapeDtypeStruct((tokens, width), jnp.bfloat16),
            jax.ShapeDtypeStruct((2 * heads, tokens), jnp.float32),
        ],
        in_specs=[SM, VM, ANY],
        out_specs=[VM, VM],
        scratch_shapes=scratch(n, heads, tokens, bl, ck),
        compiler_params=pltpu.CompilerParams(vmem_limit_bytes=VMEM_LIMIT),
        cost_estimate=pl.CostEstimate(
            flops=4 * tokens * width * n * bl, bytes_accessed=kv.size * 2, transcendentals=tokens * heads * n * bl
        ),
    )(tab, q, kv)


def causal_kernel(q_ref, k_ref, v_ref, o_ref, st_ref):
    tokens, width = q_ref.shape
    heads = width // HD
    c = HD ** (-0.5) * LOG2E
    ok = lax.broadcasted_iota(jnp.int32, (tokens, tokens), 1) <= lax.broadcasted_iota(
        jnp.int32, (tokens, tokens), 0
    )
    lane = lax.broadcasted_iota(jnp.int32, (tokens, HD), 1)
    st = jnp.zeros((tokens, HD), jnp.float32)
    for g in range(heads):
        s = lax.dot_general(
            q_ref[:, g * HD : (g + 1) * HD], k_ref[...], (((1,), (1,)), ((), ())),
            preferred_element_type=jnp.float32,
        )
        s = jnp.where(ok, s, NEG)
        m = jnp.max(s, axis=1, keepdims=True)
        p = jnp.where(ok, jnp.exp2((s - m) * c), 0.0)
        total = jnp.sum(p, axis=1, keepdims=True)
        mixed = jnp.dot(p.astype(jnp.bfloat16), v_ref[...], preferred_element_type=jnp.float32)
        o_ref[:, g * HD : (g + 1) * HD] = mixed / total
        st = jnp.where(lane == g, m, st)
        st = jnp.where(lane == heads + g, total, st)
    st_ref[...] = st.T[: 2 * heads]


def causal_attention(q, k, v):
    tokens, width = q.shape
    heads = width // HD
    return pl.pallas_call(
        causal_kernel,
        out_shape=[
            jax.ShapeDtypeStruct((tokens, width), jnp.float32),
            jax.ShapeDtypeStruct((2 * heads, tokens), jnp.float32),
        ],
        in_specs=[VM] * 3,
        out_specs=[VM] * 2,
        compiler_params=pltpu.CompilerParams(vmem_limit_bytes=VMEM_LIMIT),
        cost_estimate=pl.CostEstimate(
            flops=4 * tokens * width * tokens, bytes_accessed=tokens * width * 8, transcendentals=tokens * heads * tokens
        ),
    )(q, k, v)


def own_kernel(
    tab, q_ref, kv_hbm, op_ref, stp_ref, oc_ref, stc_ref, o_ref,
    kbuf, vbuf, acc, m_s, l_s, order, sems, *, ck, tb,
):
    reset(acc, m_s, l_s)
    prefix_pass(tab, q_ref, kv_hbm, kbuf, vbuf, acc, m_s, l_s, order, sems, ck, tb)
    heads, tokens, _ = acc.shape
    n = order.shape[0]
    c = HD ** (-0.5) * LOG2E
    fill = jnp.zeros((HD - 2 * heads, tokens), jnp.float32)
    stp = jnp.concatenate([stp_ref[...], fill], axis=0).T
    stc = jnp.concatenate([stc_ref[...], fill], axis=0).T
    alive = lax.broadcasted_iota(jnp.int32, (tokens, HD), 0) < tab[n + 1]
    for g in range(heads):
        cols = slice(g * HD, (g + 1) * HD)
        m_p, l_p = stp[:, g : g + 1], stp[:, heads + g : heads + g + 1]
        m_c, l_c = stc[:, g : g + 1], stc[:, heads + g : heads + g + 1]
        m_o = m_s[g][:, :1]
        l_o = jnp.sum(l_s[g], axis=1, keepdims=True)
        m = jnp.maximum(jnp.maximum(m_o, m_p), m_c)
        w_o = jnp.exp2((m_o - m) * c)
        w_p = l_p * jnp.exp2((m_p - m) * c)
        w_c = l_c * jnp.exp2((m_c - m) * c)
        inv = 1.0 / (l_o * w_o + w_p + w_c)
        mixed = (
            acc[g] * (w_o * inv)
            + op_ref[:, cols].astype(jnp.float32) * (w_p * inv)
            + oc_ref[:, cols] * (w_c * inv)
        )
        o_ref[:, cols] = jnp.where(alive, mixed, 0.0).astype(o_ref.dtype)


def own_attention(tab, q, kv, op, stp, oc, stc, ck=1024, tb=256):
    n, bl = tab.shape[0] - 2, kv.shape[3]
    tokens, width = q.shape
    heads = width // HD
    return pl.pallas_call(
        functools.partial(own_kernel, ck=ck, tb=tb),
        out_shape=jax.ShapeDtypeStruct((tokens, width), jnp.bfloat16),
        in_specs=[SM, VM, ANY, VM, VM, VM, VM],
        out_specs=VM,
        scratch_shapes=scratch(n, heads, tokens, bl, ck),
        compiler_params=pltpu.CompilerParams(vmem_limit_bytes=VMEM_LIMIT),
        cost_estimate=pl.CostEstimate(
            flops=4 * tokens * width * n * bl, bytes_accessed=kv.size * 2, transcendentals=tokens * heads * n * bl
        ),
    )(tab, q, kv, op, stp, oc, stc)


def gather_kernel(dest, ids, pool_ref, out_ref, sem):
    n, per = out_ref.shape[0], ids.shape[1]

    def one(i, carry):
        for k in range(per):
            pltpu.make_async_copy(pool_ref.at[ids[dest[i], k]], out_ref.at[i, k], sem).start()
        return carry

    lax.fori_loop(0, n, one, 0)
    pltpu.make_async_copy(out_ref, out_ref, sem).wait()


def gather_paged_kernel(dest, ids, pool_ref, near_ref, away_ref, out_ref, sems):
    n, per = out_ref.shape[0], ids.shape[1]
    half = near_ref.shape[1]

    def one(i, carry):
        for k in range(per):
            pltpu.make_async_copy(pool_ref.at[ids[dest[i], k]], out_ref.at[i, k], sems.at[0]).start()
        return carry

    lax.fori_loop(0, n, one, 0)
    for i in range(n):
        out_ref[i, per, 0, :half] = near_ref[i]
        out_ref[i, per, 0, half:] = away_ref[i]
        out_ref[i, per, 1] = jnp.zeros_like(out_ref[i, per, 1])
    filled = out_ref.at[:, pl.ds(0, per)]
    pltpu.make_async_copy(filled, filled, sems.at[0]).wait()


def gather_blocks(dest, ids, pool, pages=()):
    n, per = dest.shape[0], ids.shape[1]
    _, two, bl, _ = pool.shape
    return pl.pallas_call(
        gather_paged_kernel if pages else gather_kernel,
        out_shape=jax.ShapeDtypeStruct((n, per + (1 if pages else 0), two, bl, HD), pool.dtype),
        in_specs=[SM, SM, ANY] + [VM] * len(pages),
        out_specs=VM,
        scratch_shapes=[pltpu.SemaphoreType.DMA((1,)) if pages else pltpu.SemaphoreType.DMA],
        compiler_params=pltpu.CompilerParams(vmem_limit_bytes=VMEM_LIMIT),
        cost_estimate=pl.CostEstimate(flops=0, bytes_accessed=4 * n * per * two * bl * HD, transcendentals=0),
    )(dest, ids, pool, *pages)


NX, NZ, NY = 4, 2, 4
NL = 4
PG = 16


def by_rank(holders, per):
    slots = holders.shape[0]
    i = jnp.arange(slots, dtype=jnp.int32)
    same = (holders[:, None] == holders[None, :]) & (i[None, :] < i[:, None])
    place = holders * per + jnp.sum(same.astype(jnp.int32), axis=1)
    return place[None, :] == i[:, None]


def pick(hot, values):
    return jnp.sum(jnp.where(hot, values[None, :], 0), axis=1)


def local(
    queries,
    new_keys,
    new_values,
    kv_pool,
    out_weight,
    prefix_len,
    new_count,
    hit_holder,
    hit_block,
    decode_owner,
):
    slots = hit_holder.shape[1]
    n_pool = lax.axis_size("pool")
    per = slots // n_pool
    tokens, width = queries.shape
    plane_n = NX * NY
    me = lax.axis_index("pool")
    t_me = lax.axis_index("tp")
    zh = (me // NY) % NZ
    flip = [(p, p ^ NY) for p in range(n_pool)]
    planes = [[x * NZ * NY + z * NY + y for x in range(NX) for y in range(NY)] for z in range(NZ)]

    def a2a(x, groups=None):
        return lax.all_to_all(x, "pool", 0, 0, axis_index_groups=groups, tiled=True)

    hot = by_rank(hit_holder[0], per)
    slot_of = pick(hot, jnp.arange(slots, dtype=jnp.int32))
    ids = pick(hot, hit_block[0]).reshape(n_pool, per)
    ids_in = a2a(ids)
    lens = jnp.concatenate([prefix_len, new_count])
    meta = jnp.concatenate([slot_of, lens])
    q_far = lax.ppermute(queries, "pool", flip)
    meta_far = lax.ppermute(meta, "pool", flip)

    def table(info):
        grid = info[:slots].reshape(NX, NZ, NY * per)
        pos = lax.dynamic_index_in_dim(grid, zh, 1, keepdims=False).reshape(-1)
        return jnp.concatenate([pos, info[slots:]])

    keep = (jnp.arange(tokens, dtype=jnp.int32) < new_count[0])[:, None]
    both = jnp.stack([jnp.where(keep, new_keys, 0), jnp.where(keep, new_values, 0)])
    pages = decode_owner.shape[1]
    both = both.reshape(2, pages, PG, HD)
    page_of = pick(by_rank(decode_owner[0], 1), jnp.arange(pages, dtype=jnp.int32))
    ordered = jnp.transpose(both[:, page_of], (1, 0, 2, 3)).reshape(NX, NZ, NY, 2 * PG, HD)
    near = lax.dynamic_index_in_dim(ordered, zh, 1, keepdims=False).reshape(plane_n, 2 * PG, HD)
    away = lax.dynamic_index_in_dim(ordered, 1 - zh, 1, keepdims=False).reshape(plane_n, 2 * PG, HD)
    away = lax.ppermute(away, "pool", flip)

    xs, ys = jnp.arange(plane_n, dtype=jnp.int32) // NY, jnp.arange(plane_n, dtype=jnp.int32) % NY
    base = xs * (NZ * NY) + ys
    send_far = gather_blocks(base + (1 - zh) * NY, ids_in, kv_pool)
    send_own = gather_blocks(base + zh * NY, ids_in, kv_pool, (near, away))
    send_own, q_far = lax.optimization_barrier((send_own, q_far))
    got_far = a2a(send_far, planes)
    got_own = a2a(send_own, planes)

    o_c, st_c = causal_attention(queries, new_keys, new_values)
    w_other = lax.ppermute(out_weight, "tp", [(t, t ^ 1) for t in range(2 * NL)])

    tab_far = table(meta_far)
    o_far, st_far = partner_attention(tab_far, q_far, got_far, ck=1024)
    o_p = lax.ppermute(o_far, "pool", flip)
    st_p = lax.ppermute(st_far, "pool", flip)

    att = own_attention(table(meta), queries, got_own, o_p, st_p, o_c, st_c)

    core, j = t_me % 2, t_me // 2
    rows = att.reshape(NL, 2, tokens // (2 * NL), width)
    x_me = lax.dynamic_index_in_dim(rows, core, 1, keepdims=False)
    x_give = lax.dynamic_index_in_dim(rows, 1 - core, 1, keepdims=False)
    x_got = lax.ppermute(x_give, "tp", [(t, t ^ 1) for t in range(2 * NL)])
    d_out = out_weight.shape[1]
    chunk = tokens // (2 * NL)
    part = jnp.dot(x_me.reshape(-1, width), out_weight, preferred_element_type=jnp.float32)
    part = part + jnp.dot(x_got.reshape(-1, width), w_other, preferred_element_type=jnp.float32)
    part = part.astype(jnp.bfloat16).reshape(NL, chunk, d_out)

    def own_part(d):
        d = jnp.clip(d, 0, NL - 1)
        return lax.dynamic_index_in_dim(part, d, 0, keepdims=False).astype(jnp.float32)

    right = left = None
    for s in range(1, NL):
        give_r, give_l = own_part(NL - s + j), own_part(s + j - NL)
        if right is not None:
            give_r, give_l = give_r + right.astype(jnp.float32), give_l + left.astype(jnp.float32)
        hops = [(jj, jj + 1) for jj in range(s)]
        to_r = [(2 * a + k, 2 * b + k) for a, b in hops for k in range(2)]
        to_l = [(2 * (NL - 1 - a) + k, 2 * (NL - 1 - b) + k) for a, b in hops for k in range(2)]
        right = lax.ppermute(give_r.astype(jnp.bfloat16), "tp", to_r)
        left = lax.ppermute(give_l.astype(jnp.bfloat16), "tp", to_l)
    summed = own_part(j) + right.astype(jnp.float32) + left.astype(jnp.float32)

    arrived = got_own[:, per, 0].reshape(NX, NY, 2, 2 * PG, HD)
    near_in, far_in = arrived[:, :, 0], arrived[:, :, 1]
    by_z = jnp.where(zh == 0, jnp.stack([near_in, far_in], 1), jnp.stack([far_in, near_in], 1))
    decode = by_z.reshape(n_pool, 1, 2, PG, HD)[None]
    return (summed.astype(jnp.bfloat16), decode)


def solution(mesh):
    from jax.sharding import PartitionSpec as P

    in_specs = (
        P("pool", "tp"),
        P("pool", "tp"),
        P("pool", "tp"),
        P("pool", None, None, "tp"),
        P("tp", None),
        P("pool"),
        P("pool"),
        P("pool", None),
        P("pool", None),
        P("pool", None),
    )
    out_specs = (P(("pool", "tp"), None), P("pool", None, None, None, None, "tp"))
    return jax.shard_map(local, mesh=mesh, in_specs=in_specs, out_specs=out_specs, check_vma=False)
```

time: 357 us -> 221 us (0.62)
  the two profiles are of different devices: /device:TPU:28 before, /device:TPU:190 now
where the time goes in v1:
time: 221 us; the launch traced here: 217 us
  waiting for transfers between devices  83.6 us (38%)
  starting transfers between devices  56.6 us (26%)
  Pallas kernels  56.2 us (25%)
  other arithmetic  8.46 us (4%)
  matrix products  4.85 us (2%)
  local copies, waits for them, and re-layouts  4.73 us (2%)
  between operations  2.36 us (1%)
    all_to_all x3, starting transfers between devices, a2a(): return lax.all_to_all(x, 'pool', 0, 0, axis_index_groups=groups, tiled=True)  26.7 us
    ppermute x3, waiting for transfers between devices, local(): right = lax.ppermute(give_r.astype(jnp.bfloat16), 'tp', to_r)  26.2 us
    ppermute x1, waiting for transfers between devices, local(): away = lax.ppermute(away, 'pool', flip)  24.2 us
    pallas_call x1, Pallas kernels, partner_attention(): pl.pallas_call(functools.partial(partner_kernel, ck=ck, tb=tb), out_shape...  23.7 us
    pallas_call x1, Pallas kernels, own_attention(): pl.pallas_call(functools.partial(own_kernel, ck=ck, tb=tb), out_shape=jax...  23.1 us
    ppermute x3, waiting for transfers between devices, local(): left = lax.ppermute(give_l.astype(jnp.bfloat16), 'tp', to_l)  18.1 us
    ppermute x3, starting transfers between devices, local(): right = lax.ppermute(give_r.astype(jnp.bfloat16), 'tp', to_r)  7.75 us
    ppermute x1, waiting for transfers between devices, local(): st_p = lax.ppermute(st_far, 'pool', flip)  7.54 us
  transfers between devices with their start and end apart: 16, of which 9 were waited for; matrix products, arithmetic and copies ran while one was open for 2% of the time, Pallas kernels for 24%

profile of v1, /device:TPU:190, one launch (start us, length us, event | category | flops | bytes accessed | tf_op | source)
XLA Modules:
  0.0 216.8 jit_solution(17708443059696161585)
XLA Ops:
  0.6 0.9 convert_reduce_fusion
  1.5 0.7 fusion.15
  2.2 1.3 select_reduce_fusion
  3.5 0.7 all_to_all.13
  4.2 12.1 %all-to-all-start = ((s32[32,1,4]{2,1,0:T(1,128)}), s32[32,1,4]{2,1,0:T(1,128)S(1)}, u32[]{:S(2)}, u32[]{:S(2)}) async-start(s32[32,1,4]{2,1,0:T(1,128)} %bitcast.4), calls=%async_computation | async-start | bytes 32768 | tf_op jit(solution)/shard_map/all_to_all | solution.py:348
  16.4 3.8 %all-to-all-done = s32[32,1,4]{2,1,0:T(1,128)S(1)} async-done(((s32[32,1,4]{2,1,0:T(1,128)}), s32[32,1,4]{2,1,0:T(1,128)S(1)}, u32[]{:S(2)}, u32[]{:S(2)}) %all-to-all-start) | async-done | bytes 544 | tf_op jit(solution)/shard_map/all_to_all | solution.py:348
  20.2 0.1 copy.29
  20.3 0.1 copy.30.ids
  20.4 3.7 %shard_map.114 = bf16[16,4,2,64,128]{4,3,2,1,0:T(8,128)(2,1)} custom-call(s32[16]{0:T(128)S(1)} %broadcast_add_fusion.dest, s32[32,4]{1,0:T(8,128)S(1)} %copy.30.ids, bf16[192,2,64,128]{3,2,1,0:T(8,128)(2,1)} %pool_ref.3), custom_call_target="tpu_custom_call" | custom-call | bytes 4194304 | tf_op jit(solution)/shard_map/pallas_call | solution.py:296
  24.0 0.0 copy-start.2
  24.0 0.0 copy-start.5
  24.0 0.0 copy-start
  24.1 0.0 copy-start.1
  24.1 7.3 %all-to-all-start.2 = ((bf16[16,4,2,64,128]{4,3,2,1,0:T(8,128)(2,1)}), bf16[16,4,2,64,128]{4,3,2,1,0:T(8,128)(2,1)S(1)}, u32[]{:S(2)}, u32[]{:S(2)}) async-start(bf16[16,4,2,64,128]{4,3,2,1,0:T(8,128)(2,1)} %shard_map.114), calls=%async_computation.2 | async-start | bytes 4194304 | tf_op jit(solution)/shard_map/all_to_all | solution.py:348
  31.4 5.5 %collective-permute-start.1 = (bf16[512,512]{1,0:T(8,128)(2,1)S(1)}, bf16[512,512]{1,0:T(8,128)(2,1)}, u32[]{:S(2)}, u32[]{:S(2)}) collective-permute-start(bf16[512,512]{1,0:T(8,128)(2,1)S(1)} %copy-done.2), channel_id=1, source_target_pairs={{0,32},{8,40},{16,48},{24,56},{32,0},{40,8},{48,16},{56,24},{64,96... | collective-permute-start | bytes 1572872 | tf_op jit(solution)/shard_map/ppermute | solution.py:356
  37.5 0.2 convert_reduce_fusion.1
  37.7 0.1 select_reduce_fusion.2
  37.9 0.1 broadcast_select_fusion.1
  38.0 0.6 pad_clamp_fusion
  38.7 0.7 gather_fusion
  39.4 0.7 collective-permute-start
  40.1 24.2 %collective-permute-done.away_ref = bf16[16,32,128]{2,1,0:T(8,128)(2,1)S(1)} collective-permute-done((bf16[16,32,128]{2,1,0:T(8,128)(2,1)S(1)}, bf16[16,32,128]{2,1,0:T(8,128)(2,1)S(1)}, u32[]{:S(2)}, u32[]{:S(2)}) %collective-permute-start) | collective-permute-done | bytes 131104 | tf_op jit(solution)/shard_map/ppermute | solution.py:372
  64.3 3.9 %shard_map.113 = bf16[16,5,2,64,128]{4,3,2,1,0:T(8,128)(2,1)} custom-call(s32[16]{0:T(128)S(1)} %broadcast_add_fusion.1.dest, s32[32,4]{1,0:T(8,128)S(1)} %copy.30.ids, bf16[192,2,64,128]{3,2,1,0:T(8,128)(2,1)} %pool_ref.3, bf16[16,32,128]{2,1,0:T(8,128)(2,1)S(1)} %bitcast.65, bf16[16,32,128]{2,1,0:T(8,128)(2,1)S(1)} %collective-permute-done.away_ref), custom_call_target="tpu_custom_call" | custom-call | bytes 4194304 | tf_op jit(solution)/shard_map/pallas_call | solution.py:296
  68.2 0.0 copy-start.4
  68.2 0.0 all-to-all-done.2.kv_hbm
  68.2 7.2 %all-to-all-start.1 = ((bf16[16,5,2,64,128]{4,3,2,1,0:T(8,128)(2,1)}), bf16[16,5,2,64,128]{4,3,2,1,0:T(8,128)(2,1)}, u32[]{:S(2)}, u32[]{:S(2)}) async-start(bf16[16,5,2,64,128]{4,3,2,1,0:T(8,128)(2,1)} %shard_map.113), calls=%async_computation.1 | async-start | bytes 5242880 | tf_op jit(solution)/shard_map/all_to_all | solution.py:348
  76.1 0.1 pad_add_fusion
  76.2 5.3 %collective-permute-start.2 = (s32[130]{0:T(256)S(1)}, s32[130]{0:T(256)S(1)}, u32[]{:S(2)}, u32[]{:S(2)}) collective-permute-start(s32[130]{0:T(256)S(1)} %pad_add_fusion), channel_id=1, source_target_pairs={{0,32},{8,40},{16,48},{24,56},{32,0},{40,8},{48,16},{56,24},{64,96... | collective-permute-start | bytes 1568 | tf_op jit(solution)/shard_map/ppermute | solution.py:357
  81.5 2.2 %collective-permute-done.2 = s32[130]{0:T(256)S(1)} collective-permute-done((s32[130]{0:T(256)S(1)}, s32[130]{0:T(256)S(1)}, u32[]{:S(2)}, u32[]{:S(2)}) %collective-permute-start.2) | collective-permute-done | bytes 552 | tf_op jit(solution)/shard_map/ppermute | solution.py:357
  83.7 0.1 reshape.106
  83.8 0.1 reshape.107
  83.9 0.1 pad_add_fusion.2.tab
  84.0 23.7 %shard_map.115 = (bf16[512,512]{1,0:T(8,128)(2,1)}, f32[8,512]{1,0:T(8,128)S(1)}) custom-call(s32[66]{0:T(128)S(1)} %pad_add_fusion.2.tab, bf16[512,512]{1,0:T(8,128)(2,1)} %collective-permute-done.1.q_ref, bf16[16,4,2,64,128]{4,3,2,1,0:T(8,128)(2,1)S(1)} %all-to-all-done.2.kv_hbm), custom_call_target="tpu_custom_call" | custom-call | flops 4294967296 | bytes 2097152 | tf_op jit(solution)/shard_map/pallas_call | solution.py:155
  107.7 5.4 %collective-permute-start.3 = (bf16[512,512]{1,0:T(8,128)(2,1)}, bf16[512,512]{1,0:T(8,128)(2,1)S(1)}, u32[]{:S(2)}, u32[]{:S(2)}) collective-permute-start(bf16[512,512]{1,0:T(8,128)(2,1)} %get-tuple-element.10), channel_id=1, source_target_pairs={{0,32},{8,40},{16,48},{24,56},{32,0},{40,8},{48,16},{56,24},{64,96... | collective-permute-start | bytes 1572872 | tf_op jit(solution)/shard_map/ppermute | solution.py:387
  113.1 0.1 reshape.101
  113.2 0.1 reshape.102
  113.3 0.1 pad_add_fusion.1.tab
  113.4 0.7 collective-permute-start.4
  114.0 1.8 shard_map.116
  115.8 7.5 %collective-permute-done.4.stp_ref = f32[8,512]{1,0:T(8,128)S(1)} collective-permute-done((f32[8,512]{1,0:T(8,128)S(1)}, f32[8,512]{1,0:T(8,128)S(1)}, u32[]{:S(2)}, u32[]{:S(2)}) %collective-permute-start.4) | collective-permute-done | bytes 16416 | tf_op jit(solution)/shard_map/ppermute | solution.py:388
  123.3 23.1 %shard_map.117 = bf16[512,512]{1,0:T(8,128)(2,1)S(1)} custom-call(s32[66]{0:T(128)S(1)} %pad_add_fusion.1.tab, bf16[512,512]{1,0:T(8,128)(2,1)S(1)} %copy-done.2, bf16[16,5,2,64,128]{4,3,2,1,0:T(8,128)(2,1)} %all-to-all-done.1.kv_hbm, bf16[512,512]{1,0:T(8,128)(2,1)S(1)} %collective-permute-done.3.op_ref, f32[8,512]{1,0:T(8,128)S(1)} %collective-permute-done.4.stp_ref, ...), custom_call_target="tpu_custom_call" | custom-call | flops 4294967296 | bytes 2621440 | tf_op jit(solution)/shard_map/pallas_call | solution.py:250
  146.5 0.1 constant_dynamic-slice_fusion
  146.6 0.1 collective-permute-start.5
  146.7 1.5 collective-permute-done.5
  148.2 3.6 %fusion.16 = f32[256,4096]{1,0:T(8,128)S(1)} fusion(bf16[256,512]{1,0:T(8,128)(2,1)S(1)} %bitcast.75, bf16[512,4096]{1,0:T(8,128)(2,1)} %collective-permute-done.6), kind=kOutput, calls=%fused_computation.61 | convolution fusion | flops 1073741824 | bytes 8650752 | tf_op jit(solution)/shard_map/dot_general | solution.py:400
  151.8 1.3 fusion
  153.1 0.9 dynamic-slice_bitcast_fusion.1
  153.9 1.3 collective-permute-start.7
  155.2 1.5 collective-permute-start.10
  156.7 13.1 %collective-permute-done.7 = bf16[64,4096]{1,0:T(8,128)(2,1)S(1)} collective-permute-done((bf16[64,4096]{1,0:T(8,128)(2,1)S(1)}, bf16[64,4096]{1,0:T(8,128)(2,1)S(1)}, u32[]{:S(2)}, u32[]{:S(2)}) %collective-permute-start.7) | collective-permute-done | bytes 524320 | tf_op jit(solution)/shard_map/ppermute | solution.py:415
  169.8 0.1 fusion.3
  169.9 1.9 collective-permute-start.8
  171.9 0.0 collective-permute-done.10
  171.9 13.1 %collective-permute-done.8 = bf16[64,4096]{1,0:T(8,128)(2,1)S(1)} collective-permute-done((bf16[64,4096]{1,0:T(8,128)(2,1)S(1)}, bf16[64,4096]{1,0:T(8,128)(2,1)S(1)}, u32[]{:S(2)}, u32[]{:S(2)}) %collective-permute-start.8) | collective-permute-done | bytes 524320 | tf_op jit(solution)/shard_map/ppermute | solution.py:415
  184.9 2.3 %fusion.4 = (bf16[64,4096]{1,0:T(8,128)(2,1)}, bf16[64,4096]{1,0:T(8,128)(2,1)}) fusion(bf16[64,4096]{1,0:T(8,128)(2,1)S(1)} %collective-permute-done.8, bf16[4,64,4096]{2,1,0:T(8,128)(2,1)S(1)} %bitcast.69, s32[]{:T(128)S(6)} %min.23, bf16[64,4096]{1,0:T(8,128)(2,1)} %collective-permute-done.10, s32[]{:T(128)S(6)} %min.27), kind=kLoop, calls=%fused_computation.10 | loop fusion | flops 2097152 | bytes 3145736 | tf_op jit(solution)/shard_map/convert_element_type | solution.py:415
  187.2 1.3 collective-permute-start.11
  188.5 4.5 %collective-permute-start.9 = (bf16[64,4096]{1,0:T(8,128)(2,1)}, bf16[64,4096]{1,0:T(8,128)(2,1)S(1)}, u32[]{:S(2)}, u32[]{:S(2)}) collective-permute-start(bf16[64,4096]{1,0:T(8,128)(2,1)} %get-tuple-element.16), channel_id=1, source_target_pairs={{0,2},{1,3},{2,4},{3,5},{4,6},{5,7},{8,10},{9,11},{10,12},{11,13},... | collective-permute-start | bytes 1572872 | tf_op jit(solution)/shard_map/ppermute | solution.py:415
  193.0 8.4 %collective-permute-done.11 = bf16[64,4096]{1,0:T(8,128)(2,1)S(1)} collective-permute-done((bf16[64,4096]{1,0:T(8,128)(2,1)}, bf16[64,4096]{1,0:T(8,128)(2,1)S(1)}, u32[]{:S(2)}, u32[]{:S(2)}) %collective-permute-start.11) | collective-permute-done | bytes 524320 | tf_op jit(solution)/shard_map/ppermute | solution.py:416
  201.5 0.9 fusion.2
  202.4 1.9 collective-permute-start.12
  204.3 1.0 slice.22
  205.4 0.7 copy.33
  206.1 9.7 %collective-permute-done.12 = bf16[64,4096]{1,0:T(8,128)(2,1)S(1)} collective-permute-done((bf16[64,4096]{1,0:T(8,128)(2,1)}, bf16[64,4096]{1,0:T(8,128)(2,1)S(1)}, u32[]{:S(2)}, u32[]{:S(2)}) %collective-permute-start.12) | collective-permute-done | bytes 524320 | tf_op jit(solution)/shard_map/ppermute | solution.py:416
  215.8 1.0 fusion.6
  (26 shorter events, 0.2 us)
Async XLA Ops:
  4.2 16.0 %all-to-all-start = ((s32[32,1,4]{2,1,0:T(1,128)}), s32[32,1,4]{2,1,0:T(1,128)S(1)}, u32[]{:S(2)}, u32[]{:S(2)}) async-start(s32[32,1,4]{2,1,0:T(1,128)} %bitcast.4), calls=%async_computation | async-start | bytes 32768 | tf_op jit(solution)/shard_map/all_to_all | solution.py:348
  24.0 7.4 %copy-start.2 = (bf16[512,512]{1,0:T(8,128)(2,1)S(1)}, bf16[512,512]{1,0:T(8,128)(2,1)}, u32[]{:S(2)}) copy-start(bf16[512,512]{1,0:T(8,128)(2,1)} %q_ref.3) | copy-start | bytes 1572868
  24.0 13.5 %copy-start.5 = (s32[1,32]{1,0:T(1,128)S(1)}, s32[1,32]{1,0:T(1,128)}, u32[]{:S(2)}) copy-start(s32[1,32]{1,0:T(1,128)} %param.19) | copy-start | bytes 388
  24.0 13.8 %copy-start = (bf16[512,128]{1,0:T(8,128)(2,1)S(1)}, bf16[512,128]{1,0:T(8,128)(2,1)}, u32[]{:S(2)}) copy-start(bf16[512,128]{1,0:T(8,128)(2,1)} %k_ref.1) | copy-start | bytes 393220
  24.1 13.8 %copy-start.1 = (bf16[512,128]{1,0:T(8,128)(2,1)S(1)}, bf16[512,128]{1,0:T(8,128)(2,1)}, u32[]{:S(2)}) copy-start(bf16[512,128]{1,0:T(8,128)(2,1)} %v_ref.1) | copy-start | bytes 393220
  24.1 44.1 %all-to-all-start.2 = ((bf16[16,4,2,64,128]{4,3,2,1,0:T(8,128)(2,1)}), bf16[16,4,2,64,128]{4,3,2,1,0:T(8,128)(2,1)S(1)}, u32[]{:S(2)}, u32[]{:S(2)}) async-start(bf16[16,4,2,64,128]{4,3,2,1,0:T(8,128)(2,1)} %shard_map.114), calls=%async_computation.2 | async-start | bytes 4194304 | tf_op jit(solution)/shard_map/all_to_all | solution.py:348
  31.4 36.8 %collective-permute-start.1 = (bf16[512,512]{1,0:T(8,128)(2,1)S(1)}, bf16[512,512]{1,0:T(8,128)(2,1)}, u32[]{:S(2)}, u32[]{:S(2)}) collective-permute-start(bf16[512,512]{1,0:T(8,128)(2,1)S(1)} %copy-done.2), channel_id=1, source_target_pairs={{0,32},{8,40},{16,48},{24,56},{32,0},{40,8},{48,16},{56,24},{64,96... | collective-permute-start | bytes 1572872 | tf_op jit(solution)/shard_map/ppermute | solution.py:356
  36.9 111.3 %collective-permute-start.6 = (bf16[512,4096]{1,0:T(8,128)(2,1)}, bf16[512,4096]{1,0:T(8,128)(2,1)}, u32[]{:S(2)}, u32[]{:S(2)}) collective-permute-start(bf16[512,4096]{1,0:T(8,128)(2,1)} %param.14), channel_id=1, source_target_pairs={{0,1},{1,0},{2,3},{3,2},{4,5},{5,4},{6,7},{7,6},{8,9},{9,8},{10,11... | collective-permute-start | bytes 12582920 | tf_op jit(solution)/shard_map/ppermute | solution.py:383
  39.4 24.9 %collective-permute-start = (bf16[16,32,128]{2,1,0:T(8,128)(2,1)S(1)}, bf16[16,32,128]{2,1,0:T(8,128)(2,1)S(1)}, u32[]{:S(2)}, u32[]{:S(2)}) collective-permute-start(bf16[16,32,128]{2,1,0:T(8,128)(2,1)S(1)} %bitcast.79), channel_id=1, source_target_pairs={{0,32},{8,40},{16,48},{24,56},{32,0},{40,8},{48,16},{56,24},{64,96... | collective-permute-start | bytes 393224 | tf_op jit(solution)/shard_map/ppermute | solution.py:372
  68.2 7.9 %copy-start.4 = (s32[128]{0:T(128)S(1)}, s32[128]{0:T(128)}, u32[]{:S(2)}) copy-start(s32[128]{0:T(128)} %get-tuple-element.15) | copy-start | bytes 1540
  68.2 55.1 %all-to-all-start.1 = ((bf16[16,5,2,64,128]{4,3,2,1,0:T(8,128)(2,1)}), bf16[16,5,2,64,128]{4,3,2,1,0:T(8,128)(2,1)}, u32[]{:S(2)}, u32[]{:S(2)}) async-start(bf16[16,5,2,64,128]{4,3,2,1,0:T(8,128)(2,1)} %shard_map.113), calls=%async_computation.1 | async-start | bytes 5242880 | tf_op jit(solution)/shard_map/all_to_all | solution.py:348
  76.2 7.5 %collective-permute-start.2 = (s32[130]{0:T(256)S(1)}, s32[130]{0:T(256)S(1)}, u32[]{:S(2)}, u32[]{:S(2)}) collective-permute-start(s32[130]{0:T(256)S(1)} %pad_add_fusion), channel_id=1, source_target_pairs={{0,32},{8,40},{16,48},{24,56},{32,0},{40,8},{48,16},{56,24},{64,96... | collective-permute-start | bytes 1568 | tf_op jit(solution)/shard_map/ppermute | solution.py:357
  107.7 15.6 %collective-permute-start.3 = (bf16[512,512]{1,0:T(8,128)(2,1)}, bf16[512,512]{1,0:T(8,128)(2,1)S(1)}, u32[]{:S(2)}, u32[]{:S(2)}) collective-permute-start(bf16[512,512]{1,0:T(8,128)(2,1)} %get-tuple-element.10), channel_id=1, source_target_pairs={{0,32},{8,40},{16,48},{24,56},{32,0},{40,8},{48,16},{56,24},{64,96... | collective-permute-start | bytes 1572872 | tf_op jit(solution)/shard_map/ppermute | solution.py:387
  113.4 10.0 %collective-permute-start.4 = (f32[8,512]{1,0:T(8,128)S(1)}, f32[8,512]{1,0:T(8,128)S(1)}, u32[]{:S(2)}, u32[]{:S(2)}) collective-permute-start(f32[8,512]{1,0:T(8,128)S(1)} %get-tuple-element.11), channel_id=1, source_target_pairs={{0,32},{8,40},{16,48},{24,56},{32,0},{40,8},{48,16},{56,24},{64,96... | collective-permute-start | bytes 49160 | tf_op jit(solution)/shard_map/ppermute | solution.py:388
  146.6 1.6 collective-permute-start.5
  148.2 3.6 %copy-start.3 = (bf16[512,4096]{1,0:T(8,128)(2,1)S(1)}, bf16[512,4096]{1,0:T(8,128)(2,1)}, u32[]{:S(2)}) copy-start(bf16[512,4096]{1,0:T(8,128)(2,1)} %param.14) | copy-start | bytes 12582916
  153.9 15.8 %collective-permute-start.7 = (bf16[64,4096]{1,0:T(8,128)(2,1)S(1)}, bf16[64,4096]{1,0:T(8,128)(2,1)S(1)}, u32[]{:S(2)}, u32[]{:S(2)}) collective-permute-start(bf16[64,4096]{1,0:T(8,128)(2,1)S(1)} %get-tuple-element.18), channel_id=1, source_target_pairs={{0,2},{1,3},{8,10},{9,11},{16,18},{17,19},{24,26},{25,27},{32,34},... | collective-permute-start | bytes 1572872 | tf_op jit(solution)/shard_map/ppermute | solution.py:415
  155.2 16.6 %collective-permute-start.10 = (bf16[64,4096]{1,0:T(8,128)(2,1)}, bf16[64,4096]{1,0:T(8,128)(2,1)}, u32[]{:S(2)}, u32[]{:S(2)}) collective-permute-start(bf16[64,4096]{1,0:T(8,128)(2,1)} %get-tuple-element.19), channel_id=1, source_target_pairs={{6,4},{7,5},{14,12},{15,13},{22,20},{23,21},{30,28},{31,29},{38,36... | collective-permute-start | bytes 1572872 | tf_op jit(solution)/shard_map/ppermute | solution.py:416
  169.9 15.0 %collective-permute-start.8 = (bf16[64,4096]{1,0:T(8,128)(2,1)S(1)}, bf16[64,4096]{1,0:T(8,128)(2,1)S(1)}, u32[]{:S(2)}, u32[]{:S(2)}) collective-permute-start(bf16[64,4096]{1,0:T(8,128)(2,1)S(1)} %fusion.3), channel_id=1, source_target_pairs={{0,2},{1,3},{2,4},{3,5},{8,10},{9,11},{10,12},{11,13},{16,18},{17,... | collective-permute-start | bytes 1572872 | tf_op jit(solution)/shard_map/ppermute | solution.py:415
  187.2 14.3 %collective-permute-start.11 = (bf16[64,4096]{1,0:T(8,128)(2,1)}, bf16[64,4096]{1,0:T(8,128)(2,1)S(1)}, u32[]{:S(2)}, u32[]{:S(2)}) collective-permute-start(bf16[64,4096]{1,0:T(8,128)(2,1)} %get-tuple-element.17), channel_id=1, source_target_pairs={{6,4},{7,5},{4,2},{5,3},{14,12},{15,13},{12,10},{13,11},{22,20},{2... | collective-permute-start | bytes 1572872 | tf_op jit(solution)/shard_map/ppermute | solution.py:416
  188.5 17.6 %collective-permute-start.9 = (bf16[64,4096]{1,0:T(8,128)(2,1)}, bf16[64,4096]{1,0:T(8,128)(2,1)S(1)}, u32[]{:S(2)}, u32[]{:S(2)}) collective-permute-start(bf16[64,4096]{1,0:T(8,128)(2,1)} %get-tuple-element.16), channel_id=1, source_target_pairs={{0,2},{1,3},{2,4},{3,5},{4,6},{5,7},{8,10},{9,11},{10,12},{11,13},... | collective-permute-start | bytes 1572872 | tf_op jit(solution)/shard_map/ppermute | solution.py:415
  202.4 13.4 %collective-permute-start.12 = (bf16[64,4096]{1,0:T(8,128)(2,1)}, bf16[64,4096]{1,0:T(8,128)(2,1)S(1)}, u32[]{:S(2)}, u32[]{:S(2)}) collective-permute-start(bf16[64,4096]{1,0:T(8,128)(2,1)} %fusion.2), channel_id=1, source_target_pairs={{6,4},{7,5},{4,2},{5,3},{2,0},{3,1},{14,12},{15,13},{12,10},{13,11... | collective-permute-start | bytes 1572872 | tf_op jit(solution)/shard_map/ppermute | solution.py:416

commit v2 on v0

v2 whole, which is shorter than its diff:
```python
import functools

import jax
import jax.numpy as jnp
from jax import lax
from jax.experimental import pallas as pl
from jax.experimental.pallas import tpu as pltpu
from jax.sharding import PartitionSpec as P

HD = 128
PG = 16
NX, NZ, NY = 4, 2, 4
NL = 4
SENDS = ((0, 2, 3, 1), (1, 0, 2, 3), (2, 3, 1, 0), (3, 1, 0, 2))
CK = 1024
NEG = -1e30
VMEM_LIMIT = 50 * 1024 * 1024
RATE = HD ** (-0.5) * 1.4426950408889634

VM = pl.BlockSpec(memory_space=pltpu.VMEM)
SM = pl.BlockSpec(memory_space=pltpu.SMEM)
ANY = pl.BlockSpec(memory_space=pl.ANY)
PARAMS = pltpu.CompilerParams(vmem_limit_bytes=VMEM_LIMIT)


def plan_kernel(holder, block, prefix_len, new_count, out):
    n = out.shape[0]
    slots = holder.shape[1]
    per = slots // n
    hit = lax.broadcasted_iota(jnp.int32, (n, slots), 0) == holder[...]
    lane = lax.broadcasted_iota(jnp.int32, (slots, slots), 1)
    earlier = (lax.broadcasted_iota(jnp.int32, (slots, slots), 0) < lane).astype(jnp.float32)
    rank = jnp.dot(hit.astype(jnp.float32), earlier, preferred_element_type=jnp.float32)
    at = lax.broadcasted_iota(jnp.int32, (n, out.shape[1]), 1)
    spot = lax.broadcasted_iota(jnp.int32, (n, slots), 1)
    ids = jnp.broadcast_to(block[...], (n, slots))
    row = jnp.where(at == 2 * per, prefix_len[0], 0) + jnp.where(at == 2 * per + 1, new_count[0], 0)
    for k in range(per):
        one = hit & (rank == k)
        row = jnp.where(at == k, jnp.sum(jnp.where(one, ids, 0), axis=1, keepdims=True), row)
        row = jnp.where(at == per + k, jnp.sum(jnp.where(one, spot, 0), axis=1, keepdims=True), row)
    out[...] = row


def plan(hit_holder, hit_block, prefix_len, new_count, n_pool):
    return pl.pallas_call(
        plan_kernel,
        out_shape=jax.ShapeDtypeStruct((n_pool, HD), jnp.int32),
        in_specs=[VM, VM, SM, SM],
        out_specs=VM,
        cost_estimate=pl.CostEstimate(flops=2 * n_pool * HD * HD, bytes_accessed=n_pool * HD * 4, transcendentals=0),
    )(hit_holder, hit_block, prefix_len, new_count)


def block_table(info, zh, per, ranks, bl):
    grid = info[:, per : 2 * per].reshape(NX, NZ, NY, per)
    pos = lax.dynamic_index_in_dim(grid, zh, 1, keepdims=False).reshape(NX * NY, per)
    pos = pos[:, ranks[0] : ranks[1]].reshape(-1)
    n = pos.shape[0]
    i = jnp.arange(n, dtype=jnp.int32)
    code = (i // (ranks[1] - ranks[0])) * 16 + i % (ranks[1] - ranks[0])
    live = jnp.clip(info[0, 2 * per] - pos * bl, 0, bl)
    full, part = live == bl, (live > 0) & (live < bl)
    before = jnp.sum((full[None, :] & (i[None, :] < i[:, None])).astype(jnp.int32), axis=1)
    n_full = jnp.sum(full.astype(jnp.int32))
    place = jnp.where(full, before, jnp.where(part, n_full, n))
    order = jnp.sum(jnp.where(place[None, :] == i[:, None], code[None, :], 0), axis=1)
    blocks = n_full + jnp.sum(part.astype(jnp.int32))
    return jnp.concatenate([order, jnp.stack([blocks, jnp.sum(live), info[0, 2 * per + 1]])])


def gather_kernel(*refs, takes, paged):
    dest, ids, pool_ref = refs[:3]
    out_ref, sem = refs[-2:]
    n = out_ref.shape[0]

    def one(i, carry):
        for at, (which, k) in enumerate(takes):
            pltpu.make_async_copy(
                pool_ref.at[ids[dest[which, i], k]], out_ref.at[i, pl.ds(2 * at, 2)], sem.at[0]
            ).start()
        return carry

    lax.fori_loop(0, n, one, 0)
    if paged:
        near, away = refs[3:5]
        half = near.shape[1]
        for i in range(n):
            out_ref[i, 2 * len(takes), :half] = near[i]
            out_ref[i, 2 * len(takes), half:] = away[i]
    filled = out_ref.at[:, pl.ds(0, 2 * len(takes))]
    pltpu.make_async_copy(filled, filled, sem.at[0]).wait()


def gather_blocks(dest, ids, pool, takes, pages=()):
    n = dest.shape[1]
    _, two, bl, _ = pool.shape
    rows = two * len(takes) + (1 if pages else 0)
    return pl.pallas_call(
        functools.partial(gather_kernel, takes=takes, paged=bool(pages)),
        out_shape=jax.ShapeDtypeStruct((n, rows, bl, HD), pool.dtype),
        in_specs=[SM, SM, ANY] + [VM] * len(pages),
        out_specs=VM,
        scratch_shapes=[pltpu.SemaphoreType.DMA((1,))],
        compiler_params=PARAMS,
        cost_estimate=pl.CostEstimate(flops=0, bytes_accessed=4 * n * rows * bl * HD, transcendentals=0),
    )(dest, ids, pool, *pages)


def lanes(x, times):
    return x if times == 1 else jnp.concatenate([x] * times, axis=1)


def scores(q_ref, g, k):
    return lax.dot_general(
        q_ref[:, g * HD : (g + 1) * HD], k, (((1,), (1,)), ((), ())), preferred_element_type=jnp.float32
    )


def add_keys(q_ref, k, v, ok, acc, m_s, l_s):
    heads = acc.shape[0]
    width = k.shape[0] // HD
    ahead = scores(q_ref, 0, k)
    for g in range(heads):
        s = ahead
        if g + 1 < heads:
            ahead = scores(q_ref, g + 1, k)
        if ok is not None:
            s = jnp.where(ok, s, NEG)
        m_prev = m_s[g]
        m = jnp.maximum(m_prev, jnp.max(s, axis=1, keepdims=True))
        p = jnp.exp2((s - lanes(m, width)) * RATE)
        if ok is not None:
            p = jnp.where(ok, p, 0.0)
        fade = jnp.exp2((m_prev - m) * RATE)
        m_s[g] = m
        part = p[:, :HD]
        for i in range(1, width):
            part = part + p[:, i * HD : (i + 1) * HD]
        l_s[g] = fade * l_s[g] + part
        mixed = jnp.dot(p.astype(jnp.bfloat16), v, preferred_element_type=jnp.float32)
        acc[g] = fade * acc[g] + mixed


def add_prefix(tab, q_ref, kv_hbm, kv, acc, m_s, l_s, sems, first):
    n, _, bl, _ = kv.shape
    per = min(CK // bl, n)
    ck = per * bl
    blocks, keys = tab[n], tab[n + 1]
    chunks = (blocks + per - 1) // per

    def load(ci):
        def one(i, carry):
            at = ci * per + i
            code = tab[at]
            pltpu.make_async_copy(
                kv_hbm.at[code // 16, pl.ds(2 * (first + code % 16), 2)], kv.at[at], sems.at[ci]
            ).start()
            return carry

        lax.fori_loop(0, per, one, 0)

    @pl.when(chunks > 0)
    def _():
        load(0)

    def one_chunk(ci, carry):
        @pl.when(ci + 1 < chunks)
        def _():
            load(ci + 1)

        at = pl.ds(ci * per, per)
        pltpu.make_async_copy(kv.at[at], kv.at[at], sems.at[ci]).wait()
        whole = keys >= (ci + 1) * ck

        def both():
            return kv[at, 0].reshape(ck, HD), kv[at, 1].reshape(ck, HD)

        @pl.when(whole)
        def _():
            add_keys(q_ref, *both(), None, acc, m_s, l_s)

        @pl.when(jnp.logical_not(whole))
        def _():
            ok = lax.broadcasted_iota(jnp.int32, (q_ref.shape[0], ck), 1) < keys - ci * ck
            add_keys(q_ref, *both(), ok, acc, m_s, l_s)

        return carry

    lax.fori_loop(0, chunks, one_chunk, 0)


def reset(acc, m_s, l_s):
    acc[...] = jnp.zeros_like(acc)
    l_s[...] = jnp.zeros_like(l_s)
    m_s[...] = jnp.full_like(m_s, NEG)


def write_part(o_ref, st_ref, acc, m_s, l_s):
    heads = acc.shape[0]
    lane = lax.broadcasted_iota(jnp.int32, m_s.shape[1:], 1)
    st = jnp.zeros(m_s.shape[1:], jnp.float32)
    for g in range(heads):
        total = jnp.sum(l_s[g], axis=1, keepdims=True)
        inverse = 1.0 / jnp.where(total > 0, total, 1.0)
        o_ref[:, g * HD : (g + 1) * HD] = (acc[g] * inverse).astype(o_ref.dtype)
        st = jnp.where(lane == g, m_s[g], st)
        st = jnp.where(lane == heads + g, total, st)
    st_ref[...] = st.T[: 2 * heads]


def partner_kernel(tab, q_ref, kv_hbm, o_ref, st_ref, kv, acc, m_s, l_s, sems, *, first):
    reset(acc, m_s, l_s)
    add_prefix(tab, q_ref, kv_hbm, kv, acc, m_s, l_s, sems, first)
    write_part(o_ref, st_ref, acc, m_s, l_s)


def causal_kernel(q_ref, k_ref, v_ref, o_ref, st_ref, acc, m_s, l_s):
    reset(acc, m_s, l_s)
    tokens = q_ref.shape[0]
    ok = lax.broadcasted_iota(jnp.int32, (tokens, tokens), 1) <= lax.broadcasted_iota(
        jnp.int32, (tokens, tokens), 0
    )
    add_keys(q_ref, k_ref[...], v_ref[...], ok, acc, m_s, l_s)
    write_part(o_ref, st_ref, acc, m_s, l_s)


def late_kernel(
    tab, q_ref, kv_hbm, oa, sa, ob, sb, rows, keep_ref, give_ref, kv, acc, m_s, l_s, sems, out, *, first
):
    reset(acc, m_s, l_s)
    add_prefix(tab, q_ref, kv_hbm, kv, acc, m_s, l_s, sems, first)
    heads, tokens, _ = acc.shape
    fill = jnp.zeros((HD - 2 * heads, tokens), jnp.float32)
    ta = jnp.concatenate([sa[...], fill], axis=0).T
    tb = jnp.concatenate([sb[...], fill], axis=0).T
    alive = lax.broadcasted_iota(jnp.int32, (tokens, HD), 0) < tab[kv.shape[0] + 2]
    for g in range(heads):
        cols = slice(g * HD, (g + 1) * HD)
        m_a, l_a = ta[:, g : g + 1], ta[:, heads + g : heads + g + 1]
        m_b, l_b = tb[:, g : g + 1], tb[:, heads + g : heads + g + 1]
        m_o = m_s[g][:, :1]
        l_o = jnp.sum(l_s[g], axis=1, keepdims=True)
        m = jnp.maximum(jnp.maximum(m_o, m_a), m_b)
        w_o = jnp.exp2((m_o - m) * RATE)
        w_a = l_a * jnp.exp2((m_a - m) * RATE)
        w_b = l_b * jnp.exp2((m_b - m) * RATE)
        inverse = 1.0 / (l_o * w_o + w_a + w_b)
        mixed = (
            acc[g] * (w_o * inverse)
            + oa[:, cols].astype(jnp.float32) * (w_a * inverse)
            + ob[:, cols] * (w_b * inverse)
        )
        out[:, cols] = jnp.where(alive, mixed, 0.0).astype(out.dtype)
    chunk = keep_ref.shape[0] // NL
    for i in range(NL):
        at = pl.ds(i * chunk, chunk)
        keep_ref[at] = out[pl.ds(pl.multiple_of(rows[i] * chunk, chunk), chunk)]
        give_ref[at] = out[pl.ds(pl.multiple_of(rows[NL + i] * chunk, chunk), chunk)]


def state_of(heads, tokens):
    return [pltpu.VMEM((heads, tokens, HD), jnp.float32)] * 3


def causal_attention(q, k, v, out_types):
    tokens, width = q.shape
    return pl.pallas_call(
        causal_kernel,
        out_shape=out_types,
        in_specs=[VM] * 3,
        out_specs=[VM] * 2,
        scratch_shapes=state_of(width // HD, tokens),
        compiler_params=PARAMS,
        cost_estimate=pl.CostEstimate(
            flops=4 * tokens * width * tokens, bytes_accessed=8 * tokens * width, transcendentals=tokens * tokens * 4
        ),
    )(q, k, v)


def attention(body, tab, q, kv, more, more_specs, out_types, first, more_scratch=()):
    n, bl = tab.shape[0] - 3, kv.shape[2]
    tokens, width = q.shape
    heads = width // HD
    keys = n * bl
    return pl.pallas_call(
        functools.partial(body, first=first),
        out_shape=out_types,
        in_specs=[SM, VM, ANY] + more_specs,
        out_specs=[VM] * len(out_types),
        scratch_shapes=[
            pltpu.VMEM((n, 2, bl, HD), jnp.bfloat16),
            *state_of(heads, tokens),
            pltpu.SemaphoreType.DMA((max(keys // CK, 1),)),
            *more_scratch,
        ],
        compiler_params=PARAMS,
        cost_estimate=pl.CostEstimate(
            flops=4 * tokens * width * keys, bytes_accessed=keys * HD * 4, transcendentals=tokens * heads * keys
        ),
    )(tab, q, kv, *more)


def project_kernel(x_a, x_b, w_a, w_b, *outs):
    part = jnp.dot(x_a[...], w_a[...], preferred_element_type=jnp.float32)
    part = part + jnp.dot(x_b[...], w_b[...], preferred_element_type=jnp.float32)
    chunk = outs[0].shape[0]
    for i, out in enumerate(outs):
        out[...] = part[i * chunk : (i + 1) * chunk].astype(out.dtype)


def project(x_a, x_b, w_a, w_b, cols=512):
    rows, depth = x_a.shape
    width = w_a.shape[1]
    whole = pl.BlockSpec((rows, depth), lambda c: (0, 0))
    tall = pl.BlockSpec((depth, cols), lambda c: (0, c))
    return pl.pallas_call(
        project_kernel,
        grid=(width // cols,),
        out_shape=[jax.ShapeDtypeStruct((rows // NL, width), x_a.dtype)] * NL,
        in_specs=[whole, whole, tall, tall],
        out_specs=[pl.BlockSpec((rows // NL, cols), lambda c: (0, c))] * NL,
        compiler_params=PARAMS,
        cost_estimate=pl.CostEstimate(
            flops=4 * rows * depth * width, bytes_accessed=4 * depth * width + 2 * rows * width, transcendentals=0
        ),
    )(x_a, x_b, w_a, w_b)


def along_z(hops):
    return [(2 * a + k, 2 * b + k) for a, b in hops for k in range(2)]


def scatter_sum(own, for_b, for_ac, for_d):
    f32 = jnp.float32
    from_a = lax.ppermute(for_ac, "tp", along_z([(0, 1), (3, 2)]))
    from_b = lax.ppermute(for_b, "tp", along_z([(0, 2), (3, 1), (1, 0), (2, 3)]))
    from_c = lax.ppermute(for_ac, "tp", along_z([(1, 2), (2, 1)]))
    for_d = (for_d.astype(f32) + from_a.astype(f32)).astype(own.dtype)
    from_d = lax.ppermute(for_d, "tp", along_z([(0, 1), (1, 3), (3, 2), (2, 0)]))
    summed = own.astype(f32) + from_b.astype(f32) + from_c.astype(f32) + from_d.astype(f32)
    return summed.astype(own.dtype)


def local(
    queries,
    new_keys,
    new_values,
    kv_pool,
    out_weight,
    prefix_len,
    new_count,
    hit_holder,
    hit_block,
    decode_owner,
):
    n_pool = lax.axis_size("pool")
    per = hit_holder.shape[1] // n_pool
    tokens, width = queries.shape
    heads = width // HD
    bl = kv_pool.shape[2]
    plane_n = NX * NY
    me = lax.axis_index("pool")
    t_me = lax.axis_index("tp")
    zh = (me // NY) % NZ
    flip = [(p, p ^ NY) for p in range(n_pool)]
    cores = [(t, t ^ 1) for t in range(2 * NL)]
    planes = [[(x * NZ + z) * NY + y for x in range(NX) for y in range(NY)] for z in range(NZ)]

    def a2a(x, groups=None):
        return lax.all_to_all(x, "pool", 0, 0, axis_index_groups=groups, tiled=True)

    info = plan(hit_holder, hit_block, prefix_len, new_count, n_pool)
    ids = a2a(info)
    q_far = lax.ppermute(queries, "pool", flip)
    info_far = lax.ppermute(info, "pool", flip)
    w_other = lax.ppermute(out_weight, "tp", cores)

    i = jnp.arange(plane_n, dtype=jnp.int32)
    base = (i // NY) * (NZ * NY) + i % NY
    dest = jnp.stack([base + zh * NY, base + (1 - zh) * NY])
    send_a = gather_blocks(dest, ids, kv_pool, [(1, k) for k in range(per)])
    got_a = a2a(send_a, planes)

    _, owner, count, k_new, v_new, info_far, info = lax.optimization_barrier(
        (send_a, decode_owner[0], new_count, new_keys, new_values, info_far, info)
    )
    keep = (jnp.arange(tokens, dtype=jnp.int32) < count[0])[:, None]
    both = jnp.stack([jnp.where(keep, k_new, 0), jnp.where(keep, v_new, 0)])
    pages = owner.shape[0]
    both = both.reshape(2, pages, PG, HD)
    i = jnp.arange(pages, dtype=jnp.int32)
    page_of = jnp.sum(jnp.where(owner[None, :] == i[:, None], i[None, :], 0), axis=1)
    ordered = jnp.transpose(both[:, page_of], (1, 0, 2, 3)).reshape(NX, NZ, NY, 2 * PG, HD)
    near = lax.dynamic_index_in_dim(ordered, zh, 1, keepdims=False).reshape(plane_n, 2 * PG, HD)
    away = lax.dynamic_index_in_dim(ordered, 1 - zh, 1, keepdims=False).reshape(plane_n, 2 * PG, HD)
    away = lax.ppermute(away, "pool", flip)

    send_b = gather_blocks(dest, ids, kv_pool, [(0, k) for k in range(per)], (near, away))
    tab_far = block_table(info_far, zh, per, (0, per), bl)
    tab = block_table(info, zh, per, (0, per), bl)
    st_type = jax.ShapeDtypeStruct((2 * heads, tokens), jnp.float32)
    o_type = jax.ShapeDtypeStruct((tokens, width), jnp.bfloat16)
    o_wide = jax.ShapeDtypeStruct((tokens, width), jnp.float32)
    o_b, st_b = causal_attention(queries, k_new, v_new, [o_wide, st_type])
    send_b, q_far, w_other, tab_far, tab, o_b, st_b = lax.optimization_barrier(
        (send_b, q_far, w_other, tab_far, tab, o_b, st_b)
    )
    got_b = a2a(send_b, planes)

    o_far, st_far = attention(partner_kernel, tab_far, q_far, got_a, (), [], [o_type, st_type], 0)
    o_a = lax.ppermute(o_far, "pool", flip)
    st_a = lax.ppermute(st_far, "pool", flip)

    core, j = t_me % 2, t_me // 2
    mine = 2 * jnp.array(SENDS, jnp.int32)[j]
    rows = jnp.concatenate([mine + core, mine + 1 - core])
    half = jax.ShapeDtypeStruct((tokens // 2, width), jnp.bfloat16)
    x_keep, x_give = attention(
        late_kernel, tab, queries, got_b, (o_a, st_a, o_b, st_b, rows), [VM] * 4 + [SM], [half, half], 0,
        (pltpu.VMEM((tokens, width), jnp.bfloat16),),
    )
    x_got = lax.ppermute(x_give, "tp", cores)
    summed = scatter_sum(*project(x_keep, x_got, out_weight, w_other))

    arrived = got_b[:, 2 * per].reshape(NX, NY, 2, 2 * PG, HD)
    near_in, far_in = arrived[:, :, 0], arrived[:, :, 1]
    by_z = jnp.where(zh == 0, jnp.stack([near_in, far_in], 1), jnp.stack([far_in, near_in], 1))
    decode = by_z.reshape(n_pool, 1, 2, PG, HD)[None]
    return (summed, decode)


def solution(mesh):
    in_specs = (
        P("pool", "tp"),
        P("pool", "tp"),
        P("pool", "tp"),
        P("pool", None, None, "tp"),
        P("tp", None),
        P("pool"),
        P("pool"),
        P("pool", None),
        P("pool", None),
        P("pool", None),
    )
    out_specs = (P(("pool", "tp"), None), P("pool", None, None, None, None, "tp"))
    return jax.shard_map(local, mesh=mesh, in_specs=in_specs, out_specs=out_specs, check_vma=False)
```

time: 357 us -> 183 us (0.51)
  the two profiles are of different devices: /device:TPU:28 before, /device:TPU:2 now
where the time goes in v2:
time: 183 us
  waiting for transfers between devices  57 us (31%)
  Pallas kernels  53 us (29%)
  starting transfers between devices  50.2 us (27%)
  other arithmetic  10.2 us (6%)
  local copies, waits for them, and re-layouts  8.07 us (4%)
  between operations  4.81 us (3%)
    pallas_call x2, Pallas kernels, attention(): pl.pallas_call(functools.partial(body, first=first), out_shape=out_types,...  35 us
    all_to_all x3, starting transfers between devices, a2a(): return lax.all_to_all(x, 'pool', 0, 0, axis_index_groups=groups, tiled=True)  19.7 us
    ppermute x1, waiting for transfers between devices, scatter_sum(): lax.ppermute(for_d, 'tp', along_z([(0, 1), (1, 3), (3, 2), (2, 0)]))  17.4 us
    ppermute x1, waiting for transfers between devices, local(): st_a = lax.ppermute(st_far, 'pool', flip)  15.5 us
    all_to_all x3, waiting for transfers between devices, a2a(): return lax.all_to_all(x, 'pool', 0, 0, axis_index_groups=groups, tiled=True)  8.76 us
    pallas_call x2, Pallas kernels, gather_blocks(): pl.pallas_call(functools.partial(gather_kernel, takes=takes, paged=bool(p...  7.52 us
    pallas_call x1, Pallas kernels, project(): pl.pallas_call(project_kernel, grid=(width // cols,), out_shape=[jax.Shap...  7.37 us
    ppermute x1, starting transfers between devices, local(): info_far = lax.ppermute(info, 'pool', flip)  7.19 us
  transfers between devices with their start and end apart: 14, of which 8 were waited for; matrix products, arithmetic and copies ran while one was open for 8% of the time, Pallas kernels for 16%

profile of v2, /device:TPU:2, one launch (start us, length us, event | category | flops | bytes accessed | tf_op | source)
XLA Modules:
  0.0 183.3 jit_solution(15816661478644839155)
XLA Ops:
  0.6 0.1 collective-permute-start.3
  2.0 1.6 shard_map.122
  3.6 7.2 %collective-permute-start = (s32[32,128]{1,0:T(8,128)}, s32[32,128]{1,0:T(8,128)S(1)}, u32[]{:S(2)}, u32[]{:S(2)}) collective-permute-start(s32[32,128]{1,0:T(8,128)} %shard_map.122), channel_id=1, source_target_pairs={{0,32},{8,40},{16,48},{24,56},{32,0},{40,8},{48,16},{56,24},{64,96... | collective-permute-start | bytes 49160 | tf_op jit(solution)/shard_map/ppermute | solution.py:376
  10.8 7.6 %all-to-all-start = ((s32[32,1,128]{2,1,0:T(1,128)}), s32[32,1,128]{2,1,0:T(1,128)S(1)}, u32[]{:S(2)}, u32[]{:S(2)}) async-start(s32[32,1,128]{2,1,0:T(1,128)} %bitcast.54), calls=%async_computation | async-start | bytes 32768 | tf_op jit(solution)/shard_map/all_to_all | solution.py:371
  18.4 5.5 %collective-permute-start.2 = (bf16[512,512]{1,0:T(8,128)(2,1)}, bf16[512,512]{1,0:T(8,128)(2,1)}, u32[]{:S(2)}, u32[]{:S(2)}) collective-permute-start(bf16[512,512]{1,0:T(8,128)(2,1)} %q_ref.3), channel_id=1, source_target_pairs={{0,32},{8,40},{16,48},{24,56},{32,0},{40,8},{48,16},{56,24},{64,96... | collective-permute-start | bytes 1572872 | tf_op jit(solution)/shard_map/ppermute | solution.py:375
  23.9 5.4 %all-to-all-done = s32[32,1,128]{2,1,0:T(1,128)S(1)} async-done(((s32[32,1,128]{2,1,0:T(1,128)}), s32[32,1,128]{2,1,0:T(1,128)S(1)}, u32[]{:S(2)}, u32[]{:S(2)}) %all-to-all-start) | async-done | bytes 16416 | tf_op jit(solution)/shard_map/all_to_all | solution.py:371
  29.4 3.7 %shard_map.123 = bf16[16,8,64,128]{3,2,1,0:T(8,128)(2,1)} custom-call(s32[2,16]{1,0:T(2,128)S(1)} %pad_add_fusion.refs_0_, s32[32,128]{1,0:T(8,128)S(1)} %bitcast.47, bf16[192,2,64,128]{3,2,1,0:T(8,128)(2,1)} %refs_2_.3), custom_call_target="tpu_custom_call" | custom-call | bytes 4194304 | tf_op jit(solution)/shard_map/pallas_call | solution.py:99
  33.1 5.1 %all-to-all-start.2 = ((bf16[16,8,64,128]{3,2,1,0:T(8,128)(2,1)}), bf16[16,8,64,128]{3,2,1,0:T(8,128)(2,1)S(1)}, u32[]{:S(2)}, u32[]{:S(2)}) async-start(bf16[16,8,64,128]{3,2,1,0:T(8,128)(2,1)} %shard_map.123), calls=%async_computation.2 | async-start | bytes 4194304 | tf_op jit(solution)/shard_map/all_to_all | solution.py:371
  38.2 0.1 slice.28
  38.2 0.1 copy.49
  38.4 0.1 slice.31
  38.4 0.1 copy.50
  38.6 0.7 fusion.9
  39.2 0.7 broadcast_compare_fusion.1
  39.9 0.1 copy.40
  40.0 0.1 eq.78
  40.1 0.1 select_reduce_fusion.2
  40.3 0.1 broadcast_select_fusion.1
  40.4 0.7 pad_maximum_fusion
  41.2 1.6 gather_fusion
  42.7 0.6 fusion.8
  43.3 1.4 convert_reduce_fusion.2
  44.8 0.6 broadcast_select_fusion.3
  45.4 0.6 broadcast_select_fusion.2
  46.1 0.1 convert_reduce_fusion.1
  47.5 0.1 copy.41
  47.6 0.1 reshape.230
  47.7 0.1 copy.43
  47.8 0.1 eq.82
  47.9 0.1 copy.44
  48.0 0.1 reshape.233
  48.1 0.7 collective-permute-start.1
  48.8 0.1 convert_reduce_fusion
  48.9 0.1 select_reduce_fusion
  49.0 1.4 pad_add_fusion.1.tab
  50.4 1.6 shard_map.125
  52.0 1.0 copy-done.3
  54.3 1.3 pad_add_fusion.2.tab
  55.6 1.8 collective-permute-done.1.refs_4_
  57.4 3.8 %shard_map.124 = bf16[16,9,64,128]{3,2,1,0:T(8,128)(2,1)} custom-call(s32[2,16]{1,0:T(2,128)S(1)} %pad_add_fusion.refs_0_, s32[32,128]{1,0:T(8,128)S(1)} %bitcast.48, bf16[192,2,64,128]{3,2,1,0:T(8,128)(2,1)} %refs_2_.3, bf16[16,32,128]{2,1,0:T(8,128)(2,1)S(1)} %bitcast.46, bf16[16,32,128]{2,1,0:T(8,128)(2,1)S(1)} %collective-permute-done.1.refs_4_), custom_call_target="tpu_custom_call" | custom-call | bytes 4718592 | tf_op jit(solution)/shard_map/pallas_call | solution.py:99
  61.2 3.3 %all-to-all-done.2.kv_hbm = bf16[16,8,64,128]{3,2,1,0:T(8,128)(2,1)S(1)} async-done(((bf16[16,8,64,128]{3,2,1,0:T(8,128)(2,1)}), bf16[16,8,64,128]{3,2,1,0:T(8,128)(2,1)S(1)}, u32[]{:S(2)}, u32[]{:S(2)}) %all-to-all-start.2) | async-done | bytes 2097184 | tf_op jit(solution)/shard_map/all_to_all | solution.py:371
  64.6 7.0 %all-to-all-start.1 = ((bf16[16,9,64,128]{3,2,1,0:T(8,128)(2,1)}), bf16[16,9,64,128]{3,2,1,0:T(8,128)(2,1)}, u32[]{:S(2)}, u32[]{:S(2)}) async-start(bf16[16,9,64,128]{3,2,1,0:T(8,128)(2,1)} %shard_map.124), calls=%async_computation.1 | async-start | bytes 4718592 | tf_op jit(solution)/shard_map/all_to_all | solution.py:371
  71.6 18.1 %shard_map.126 = (bf16[512,512]{1,0:T(8,128)(2,1)}, f32[8,512]{1,0:T(8,128)S(1)}) custom-call(s32[67]{0:T(128)S(1)} %pad_add_fusion.1.tab, bf16[512,512]{1,0:T(8,128)(2,1)} %collective-permute-done.2.q_ref, bf16[16,8,64,128]{3,2,1,0:T(8,128)(2,1)S(1)} %all-to-all-done.2.kv_hbm), custom_call_target="tpu_custom_call" | custom-call | flops 4294967296 | bytes 2097152 | tf_op jit(solution)/shard_map/pallas_call | solution.py:286
  89.7 0.1 collective-permute-start.4
  89.8 0.7 add_bitcast_fusion
  90.5 5.9 %collective-permute-start.5 = (f32[8,512]{1,0:T(8,128)S(1)}, f32[8,512]{1,0:T(8,128)S(1)}, u32[]{:S(2)}, u32[]{:S(2)}) collective-permute-start(f32[8,512]{1,0:T(8,128)S(1)} %get-tuple-element.38), channel_id=1, source_target_pairs={{0,32},{8,40},{16,48},{24,56},{32,0},{40,8},{48,16},{56,24},{64,96... | collective-permute-start | bytes 49160 | tf_op jit(solution)/shard_map/ppermute | solution.py:413
  96.4 0.1 pad_add_fusion.3.rows
  96.5 15.5 %collective-permute-done.5.sa = f32[8,512]{1,0:T(8,128)S(1)} collective-permute-done((f32[8,512]{1,0:T(8,128)S(1)}, f32[8,512]{1,0:T(8,128)S(1)}, u32[]{:S(2)}, u32[]{:S(2)}) %collective-permute-start.5) | collective-permute-done | bytes 16416 | tf_op jit(solution)/shard_map/ppermute | solution.py:413
  112.0 1.2 copy-done.4
  113.2 16.9 %shard_map.127 = (bf16[256,512]{1,0:T(8,128)(2,1)S(1)}, bf16[256,512]{1,0:T(8,128)(2,1)S(1)}) custom-call(s32[67]{0:T(128)S(1)} %pad_add_fusion.2.tab, bf16[512,512]{1,0:T(8,128)(2,1)S(1)} %copy-done.2, bf16[16,9,64,128]{3,2,1,0:T(8,128)(2,1)} %all-to-all-done.1.kv_hbm, bf16[512,512]{1,0:T(8,128)(2,1)S(1)} %collective-permute-done.4.oa, ...), custom_call_target="tpu_custom_call" | custom-call | flops 4294967296 | bytes 2097152 | tf_op jit(solution)/shard_map/pallas_call | solution.py:286
  130.1 0.1 collective-permute-start.6
  130.2 1.5 collective-permute-done.6.x_b
  131.8 7.4 %shard_map.128 = (bf16[64,4096]{1,0:T(8,128)(2,1)S(1)}, bf16[64,4096]{1,0:T(8,128)(2,1)S(1)}, bf16[64,4096]{1,0:T(8,128)(2,1)S(1)}, bf16[64,4096]{1,0:T(8,128)(2,1)S(1)}) custom-call(bf16[256,512]{1,0:T(8,128)(2,1)S(1)} %get-tuple-element.41.x_a, bf16[256,512]{1,0:T(8,128)(2,1)S(1)} %collective-permute-done.6.x_b, bf16[512,4096]{1,0:T(8,128)(2,1)} %w_a.1, ...), custom_call_target="tpu_custom_call" | custom-call | flops 2147483648 | bytes 10485760 | tf_op jit(solution)/shard_map/pallas_call | solution.py:317
  139.1 2.2 %collective-permute-start.9 = (bf16[64,4096]{1,0:T(8,128)(2,1)S(1)}, bf16[64,4096]{1,0:T(8,128)(2,1)S(1)}, u32[]{:S(2)}, u32[]{:S(2)}) collective-permute-start(bf16[64,4096]{1,0:T(8,128)(2,1)S(1)} %get-tuple-element.46), channel_id=1, source_target_pairs={{0,2},{1,3},{6,4},{7,5},{8,10},{9,11},{14,12},{15,13},{16,18},{17,... | collective-permute-start | bytes 1572872 | tf_op jit(solution)/shard_map/ppermute | solution.py:336
  141.4 0.7 collective-permute-start.8
  142.1 5.7 %collective-permute-start.7 = (bf16[64,4096]{1,0:T(8,128)(2,1)S(1)}, bf16[64,4096]{1,0:T(8,128)(2,1)S(1)}, u32[]{:S(2)}, u32[]{:S(2)}) collective-permute-start(bf16[64,4096]{1,0:T(8,128)(2,1)S(1)} %get-tuple-element.45), channel_id=1, source_target_pairs={{0,4},{1,5},{6,2},{7,3},{2,0},{3,1},{4,6},{5,7},{8,12},{9,13},{14,... | collective-permute-start | bytes 1572872 | tf_op jit(solution)/shard_map/ppermute | solution.py:337
  147.7 5.9 %collective-permute-done.9 = bf16[64,4096]{1,0:T(8,128)(2,1)S(1)} collective-permute-done((bf16[64,4096]{1,0:T(8,128)(2,1)S(1)}, bf16[64,4096]{1,0:T(8,128)(2,1)S(1)}, u32[]{:S(2)}, u32[]{:S(2)}) %collective-permute-start.9) | collective-permute-done | bytes 524320 | tf_op jit(solution)/shard_map/ppermute | solution.py:336
  153.6 0.9 add_convert_fusion.1
  154.5 2.5 %collective-permute-start.10 = (bf16[64,4096]{1,0:T(8,128)(2,1)}, bf16[64,4096]{1,0:T(8,128)(2,1)S(1)}, u32[]{:S(2)}, u32[]{:S(2)}) collective-permute-start(bf16[64,4096]{1,0:T(8,128)(2,1)} %add_convert_fusion.1), channel_id=1, source_target_pairs={{0,2},{1,3},{2,6},{3,7},{6,4},{7,5},{4,0},{5,1},{8,10},{9,11},{10,... | collective-permute-start | bytes 1572872 | tf_op jit(solution)/shard_map/ppermute | solution.py:340
  157.0 1.0 slice.38
  158.0 0.7 copy.46
  158.8 6.1 %collective-permute-done.7 = bf16[64,4096]{1,0:T(8,128)(2,1)S(1)} collective-permute-done((bf16[64,4096]{1,0:T(8,128)(2,1)S(1)}, bf16[64,4096]{1,0:T(8,128)(2,1)S(1)}, u32[]{:S(2)}, u32[]{:S(2)}) %collective-permute-start.7) | collective-permute-done | bytes 524320 | tf_op jit(solution)/shard_map/ppermute | solution.py:337
  164.9 17.4 %collective-permute-done.10 = bf16[64,4096]{1,0:T(8,128)(2,1)S(1)} collective-permute-done((bf16[64,4096]{1,0:T(8,128)(2,1)}, bf16[64,4096]{1,0:T(8,128)(2,1)S(1)}, u32[]{:S(2)}, u32[]{:S(2)}) %collective-permute-start.10) | collective-permute-done | bytes 524320 | tf_op jit(solution)/shard_map/ppermute | solution.py:340
  182.3 1.1 add_convert_fusion
  (33 shorter events, 0.2 us)
Async XLA Ops:
  0.6 60.6 %collective-permute-start.3 = (bf16[512,4096]{1,0:T(8,128)(2,1)}, bf16[512,4096]{1,0:T(8,128)(2,1)}, u32[]{:S(2)}, u32[]{:S(2)}) collective-permute-start(bf16[512,4096]{1,0:T(8,128)(2,1)} %w_a.1), channel_id=1, source_target_pairs={{0,1},{1,0},{2,3},{3,2},{4,5},{5,4},{6,7},{7,6},{8,9},{9,8},{10,11... | collective-permute-start | bytes 12582920 | tf_op jit(solution)/shard_map/ppermute | solution.py:377
  3.6 34.6 %collective-permute-start = (s32[32,128]{1,0:T(8,128)}, s32[32,128]{1,0:T(8,128)S(1)}, u32[]{:S(2)}, u32[]{:S(2)}) collective-permute-start(s32[32,128]{1,0:T(8,128)} %shard_map.122), channel_id=1, source_target_pairs={{0,32},{8,40},{16,48},{24,56},{32,0},{40,8},{48,16},{56,24},{64,96... | collective-permute-start | bytes 49160 | tf_op jit(solution)/shard_map/ppermute | solution.py:376
  10.8 18.6 %all-to-all-start = ((s32[32,1,128]{2,1,0:T(1,128)}), s32[32,1,128]{2,1,0:T(1,128)S(1)}, u32[]{:S(2)}, u32[]{:S(2)}) async-start(s32[32,1,128]{2,1,0:T(1,128)} %bitcast.54), calls=%async_computation | async-start | bytes 32768 | tf_op jit(solution)/shard_map/all_to_all | solution.py:371
  18.4 42.8 %collective-permute-start.2 = (bf16[512,512]{1,0:T(8,128)(2,1)}, bf16[512,512]{1,0:T(8,128)(2,1)}, u32[]{:S(2)}, u32[]{:S(2)}) collective-permute-start(bf16[512,512]{1,0:T(8,128)(2,1)} %q_ref.3), channel_id=1, source_target_pairs={{0,32},{8,40},{16,48},{24,56},{32,0},{40,8},{48,16},{56,24},{64,96... | collective-permute-start | bytes 1572872 | tf_op jit(solution)/shard_map/ppermute | solution.py:375
  33.0 5.3 %copy-start.5 = (s32[32,128]{1,0:T(8,128)S(1)}, s32[32,128]{1,0:T(8,128)}, u32[]{:S(2)}) copy-start(s32[32,128]{1,0:T(8,128)} %shard_map.122) | copy-start | bytes 49156
  33.1 7.1 %copy-start.6 = (s32[1,32]{1,0:T(1,128)S(1)}, s32[1,32]{1,0:T(1,128)}, u32[]{:S(2)}) copy-start(s32[1,32]{1,0:T(1,128)} %param.20) | copy-start | bytes 388
  33.1 7.2 %copy-start = (bf16[512,128]{1,0:T(8,128)(2,1)S(1)}, bf16[512,128]{1,0:T(8,128)(2,1)}, u32[]{:S(2)}) copy-start(bf16[512,128]{1,0:T(8,128)(2,1)} %k_ref) | copy-start | bytes 393220
  33.1 7.2 %copy-start.1 = (bf16[512,128]{1,0:T(8,128)(2,1)S(1)}, bf16[512,128]{1,0:T(8,128)(2,1)}, u32[]{:S(2)}) copy-start(bf16[512,128]{1,0:T(8,128)(2,1)} %v_ref) | copy-start | bytes 393220
  33.1 17.3 %copy-start.2 = (bf16[512,512]{1,0:T(8,128)(2,1)S(1)}, bf16[512,512]{1,0:T(8,128)(2,1)}, u32[]{:S(2)}) copy-start(bf16[512,512]{1,0:T(8,128)(2,1)} %q_ref.3) | copy-start | bytes 1572868
  33.1 31.5 %all-to-all-start.2 = ((bf16[16,8,64,128]{3,2,1,0:T(8,128)(2,1)}), bf16[16,8,64,128]{3,2,1,0:T(8,128)(2,1)S(1)}, u32[]{:S(2)}, u32[]{:S(2)}) async-start(bf16[16,8,64,128]{3,2,1,0:T(8,128)(2,1)} %shard_map.123), calls=%async_computation.2 | async-start | bytes 4194304 | tf_op jit(solution)/shard_map/all_to_all | solution.py:371
  48.1 9.2 %collective-permute-start.1 = (bf16[16,32,128]{2,1,0:T(8,128)(2,1)S(1)}, bf16[16,32,128]{2,1,0:T(8,128)(2,1)S(1)}, u32[]{:S(2)}, u32[]{:S(2)}) collective-permute-start(bf16[16,32,128]{2,1,0:T(8,128)(2,1)S(1)} %bitcast.55), channel_id=1, source_target_pairs={{0,32},{8,40},{16,48},{24,56},{32,0},{40,8},{48,16},{56,24},{64,96... | collective-permute-start | bytes 393224 | tf_op jit(solution)/shard_map/ppermute | solution.py:397
  52.0 1.0 copy-start.3
  64.6 47.4 %all-to-all-start.1 = ((bf16[16,9,64,128]{3,2,1,0:T(8,128)(2,1)}), bf16[16,9,64,128]{3,2,1,0:T(8,128)(2,1)}, u32[]{:S(2)}, u32[]{:S(2)}) async-start(bf16[16,9,64,128]{3,2,1,0:T(8,128)(2,1)} %shard_map.124), calls=%async_computation.1 | async-start | bytes 4718592 | tf_op jit(solution)/shard_map/all_to_all | solution.py:371
  89.7 22.3 %collective-permute-start.4 = (bf16[512,512]{1,0:T(8,128)(2,1)}, bf16[512,512]{1,0:T(8,128)(2,1)S(1)}, u32[]{:S(2)}, u32[]{:S(2)}) collective-permute-start(bf16[512,512]{1,0:T(8,128)(2,1)} %get-tuple-element.37), channel_id=1, source_target_pairs={{0,32},{8,40},{16,48},{24,56},{32,0},{40,8},{48,16},{56,24},{64,96... | collective-permute-start | bytes 1572872 | tf_op jit(solution)/shard_map/ppermute | solution.py:412
  90.5 21.5 %collective-permute-start.5 = (f32[8,512]{1,0:T(8,128)S(1)}, f32[8,512]{1,0:T(8,128)S(1)}, u32[]{:S(2)}, u32[]{:S(2)}) collective-permute-start(f32[8,512]{1,0:T(8,128)S(1)} %get-tuple-element.38), channel_id=1, source_target_pairs={{0,32},{8,40},{16,48},{24,56},{32,0},{40,8},{48,16},{56,24},{64,96... | collective-permute-start | bytes 49160 | tf_op jit(solution)/shard_map/ppermute | solution.py:413
  112.0 1.2 copy-start.4
  130.1 1.6 collective-permute-start.6
  139.1 14.5 %collective-permute-start.9 = (bf16[64,4096]{1,0:T(8,128)(2,1)S(1)}, bf16[64,4096]{1,0:T(8,128)(2,1)S(1)}, u32[]{:S(2)}, u32[]{:S(2)}) collective-permute-start(bf16[64,4096]{1,0:T(8,128)(2,1)S(1)} %get-tuple-element.46), channel_id=1, source_target_pairs={{0,2},{1,3},{6,4},{7,5},{8,10},{9,11},{14,12},{15,13},{16,18},{17,... | collective-permute-start | bytes 1572872 | tf_op jit(solution)/shard_map/ppermute | solution.py:336
  141.4 23.5 %collective-permute-start.8 = (bf16[64,4096]{1,0:T(8,128)(2,1)S(1)}, bf16[64,4096]{1,0:T(8,128)(2,1)S(1)}, u32[]{:S(2)}, u32[]{:S(2)}) collective-permute-start(bf16[64,4096]{1,0:T(8,128)(2,1)S(1)} %get-tuple-element.46), channel_id=1, source_target_pairs={{2,4},{3,5},{4,2},{5,3},{10,12},{11,13},{12,10},{13,11},{18,20},{1... | collective-permute-start | bytes 1572872 | tf_op jit(solution)/shard_map/ppermute | solution.py:338
  142.1 22.8 %collective-permute-start.7 = (bf16[64,4096]{1,0:T(8,128)(2,1)S(1)}, bf16[64,4096]{1,0:T(8,128)(2,1)S(1)}, u32[]{:S(2)}, u32[]{:S(2)}) collective-permute-start(bf16[64,4096]{1,0:T(8,128)(2,1)S(1)} %get-tuple-element.45), channel_id=1, source_target_pairs={{0,4},{1,5},{6,2},{7,3},{2,0},{3,1},{4,6},{5,7},{8,12},{9,13},{14,... | collective-permute-start | bytes 1572872 | tf_op jit(solution)/shard_map/ppermute | solution.py:337
  154.5 27.8 %collective-permute-start.10 = (bf16[64,4096]{1,0:T(8,128)(2,1)}, bf16[64,4096]{1,0:T(8,128)(2,1)S(1)}, u32[]{:S(2)}, u32[]{:S(2)}) collective-permute-start(bf16[64,4096]{1,0:T(8,128)(2,1)} %add_convert_fusion.1), channel_id=1, source_target_pairs={{0,2},{1,3},{2,6},{3,7},{6,4},{7,5},{4,0},{5,1},{8,10},{9,11},{10,... | collective-permute-start | bytes 1572872 | tf_op jit(solution)/shard_map/ppermute | solution.py:340

commit v3 on v2

--- a/solution.py
+++ b/solution.py
@@ -14,13 +14,13 @@
 SENDS = ((0, 2, 3, 1), (1, 0, 2, 3), (2, 3, 1, 0), (3, 1, 0, 2))
 CK = 1024
 NEG = -1e30
-VMEM_LIMIT = 50 * 1024 * 1024
 RATE = HD ** (-0.5) * 1.4426950408889634
 
 VM = pl.BlockSpec(memory_space=pltpu.VMEM)
 SM = pl.BlockSpec(memory_space=pltpu.SMEM)
 ANY = pl.BlockSpec(memory_space=pl.ANY)
-PARAMS = pltpu.CompilerParams(vmem_limit_bytes=VMEM_LIMIT)
+LARGE = pltpu.CompilerParams(vmem_limit_bytes=62 * 1024 * 1024)
+SMALL = pltpu.CompilerParams(vmem_limit_bytes=24 * 1024 * 1024)
 
 
 def plan_kernel(holder, block, prefix_len, new_count, out):
@@ -102,7 +102,7 @@
         in_specs=[SM, SM, ANY] + [VM] * len(pages),
         out_specs=VM,
         scratch_shapes=[pltpu.SemaphoreType.DMA((1,))],
-        compiler_params=PARAMS,
+        compiler_params=LARGE,
         cost_estimate=pl.CostEstimate(flops=0, bytes_accessed=4 * n * rows * bl * HD, transcendentals=0),
     )(dest, ids, pool, *pages)
 
@@ -142,33 +142,32 @@
         acc[g] = fade * acc[g] + mixed
 
 
-def add_prefix(tab, q_ref, kv_hbm, kv, acc, m_s, l_s, sems, first):
+def load_chunk(tab, kv_in, kv, sems, ci):
+    n, _, bl, _ = kv.shape
+    per = min(CK // bl, n)
+
+    def one(i, carry):
+        at = ci * per + i
+        code = tab[at]
+        pltpu.make_async_copy(
+            kv_in.at[code // 16, pl.ds(2 * (code % 16), 2)], kv.at[at], sems.at[ci]
+        ).start()
+        return carry
+
+    @pl.when(ci * per < tab[n])
+    def _():
+        lax.fori_loop(0, per, one, 0)
+
+
+def add_prefix(tab, q_ref, kv_in, kv, acc, m_s, l_s, sems):
     n, _, bl, _ = kv.shape
     per = min(CK // bl, n)
     ck = per * bl
     blocks, keys = tab[n], tab[n + 1]
     chunks = (blocks + per - 1) // per
 
-    def load(ci):
-        def one(i, carry):
-            at = ci * per + i
-            code = tab[at]
-            pltpu.make_async_copy(
-                kv_hbm.at[code // 16, pl.ds(2 * (first + code % 16), 2)], kv.at[at], sems.at[ci]
-            ).start()
-            return carry
-
-        lax.fori_loop(0, per, one, 0)
-
-    @pl.when(chunks > 0)
-    def _():
-        load(0)
-
     def one_chunk(ci, carry):
-        @pl.when(ci + 1 < chunks)
-        def _():
-            load(ci + 1)
-
+        load_chunk(tab, kv_in, kv, sems, ci + 1)
         at = pl.ds(ci * per, per)
         pltpu.make_async_copy(kv.at[at], kv.at[at], sems.at[ci]).wait()
         whole = keys >= (ci + 1) * ck
@@ -197,130 +196,162 @@
 
 
 def write_part(o_ref, st_ref, acc, m_s, l_s):
-    heads = acc.shape[0]
-    lane = lax.broadcasted_iota(jnp.int32, m_s.shape[1:], 1)
-    st = jnp.zeros(m_s.shape[1:], jnp.float32)
+    heads, tokens, _ = acc.shape
+    lane = lax.broadcasted_iota(jnp.int32, (tokens, HD), 1)
+    st = jnp.zeros((tokens, HD), jnp.float32)
     for g in range(heads):
         total = jnp.sum(l_s[g], axis=1, keepdims=True)
         inverse = 1.0 / jnp.where(total > 0, total, 1.0)
         o_ref[:, g * HD : (g + 1) * HD] = (acc[g] * inverse).astype(o_ref.dtype)
         st = jnp.where(lane == g, m_s[g], st)
         st = jnp.where(lane == heads + g, total, st)
-    st_ref[...] = st.T[: 2 * heads]
-
-
-def partner_kernel(tab, q_ref, kv_hbm, o_ref, st_ref, kv, acc, m_s, l_s, sems, *, first):
+    st_ref[...] = st.T[: 2 * heads] if st_ref.shape[0] == 2 * heads else st
+
+
+def begin(tab, q_in, kv_in, q, kv, acc, m_s, l_s, sems):
+    copy = pltpu.make_async_copy(q_in, q, sems.at[sems.shape[0] - 1])
+    copy.start()
+    load_chunk(tab, kv_in, kv, sems, 0)
     reset(acc, m_s, l_s)
-    add_prefix(tab, q_ref, kv_hbm, kv, acc, m_s, l_s, sems, first)
+    copy.wait()
+
+
+def partner_kernel(tab, q_in, kv_in, o_ref, st_ref, q, kv, acc, m_s, l_s, sems):
+    begin(tab, q_in, kv_in, q, kv, acc, m_s, l_s, sems)
+    add_prefix(tab, q, kv_in, kv, acc, m_s, l_s, sems)
     write_part(o_ref, st_ref, acc, m_s, l_s)
 
 
-def causal_kernel(q_ref, k_ref, v_ref, o_ref, st_ref, acc, m_s, l_s):
-    reset(acc, m_s, l_s)
-    tokens = q_ref.shape[0]
+def own_kernel(tab, q_in, kv_in, k_ref, v_ref, o_ref, st_ref, q, kv, acc, m_s, l_s, sems):
+    begin(tab, q_in, kv_in, q, kv, acc, m_s, l_s, sems)
+    tokens = q.shape[0]
     ok = lax.broadcasted_iota(jnp.int32, (tokens, tokens), 1) <= lax.broadcasted_iota(
         jnp.int32, (tokens, tokens), 0
     )
-    add_keys(q_ref, k_ref[...], v_ref[...], ok, acc, m_s, l_s)
+    add_keys(q, k_ref[...], v_ref[...], ok, acc, m_s, l_s)
+    add_prefix(tab, q, kv_in, kv, acc, m_s, l_s, sems)
     write_part(o_ref, st_ref, acc, m_s, l_s)
 
 
-def late_kernel(
-    tab, q_ref, kv_hbm, oa, sa, ob, sb, rows, keep_ref, give_ref, kv, acc, m_s, l_s, sems, out, *, first
-):
-    reset(acc, m_s, l_s)
-    add_prefix(tab, q_ref, kv_hbm, kv, acc, m_s, l_s, sems, first)
-    heads, tokens, _ = acc.shape
-    fill = jnp.zeros((HD - 2 * heads, tokens), jnp.float32)
-    ta = jnp.concatenate([sa[...], fill], axis=0).T
-    tb = jnp.concatenate([sb[...], fill], axis=0).T
-    alive = lax.broadcasted_iota(jnp.int32, (tokens, HD), 0) < tab[kv.shape[0] + 2]
+def fold(parts, g, heads):
+    m = functools.reduce(jnp.maximum, [m_i for _, m_i, _ in parts])
+    shares = [l_i * jnp.exp2((m_i - m) * RATE) for _, m_i, l_i in parts]
+    total = functools.reduce(jnp.add, shares)
+    inverse = 1.0 / total
+    mixed = functools.reduce(jnp.add, [o_i * (w * inverse) for (o_i, _, _), w in zip(parts, shares)])
+    return mixed, m, total
+
+
+def columns(st_ref):
+    rows, tokens = st_ref.shape
+    return jnp.concatenate([st_ref[...], jnp.zeros((HD - rows, tokens), jnp.float32)], axis=0).T
+
+
+def stored(o_ref, st, g, heads):
+    return (
+        o_ref[:, g * HD : (g + 1) * HD].astype(jnp.float32),
+        st[:, g : g + 1],
+        st[:, heads + g : heads + g + 1],
+    )
+
+
+def merge_kernel(rows, count, oa, sa, ob, sb, *refs):
+    outs, out = refs[:-1], refs[-1]
+    tokens, width = oa.shape
+    heads = width // HD
+    ta, tb = columns(sa), sb[...]
+    alive = lax.broadcasted_iota(jnp.int32, (tokens, HD), 0) < count[0]
     for g in range(heads):
-        cols = slice(g * HD, (g + 1) * HD)
-        m_a, l_a = ta[:, g : g + 1], ta[:, heads + g : heads + g + 1]
-        m_b, l_b = tb[:, g : g + 1], tb[:, heads + g : heads + g + 1]
-        m_o = m_s[g][:, :1]
-        l_o = jnp.sum(l_s[g], axis=1, keepdims=True)
-        m = jnp.maximum(jnp.maximum(m_o, m_a), m_b)
-        w_o = jnp.exp2((m_o - m) * RATE)
-        w_a = l_a * jnp.exp2((m_a - m) * RATE)
-        w_b = l_b * jnp.exp2((m_b - m) * RATE)
-        inverse = 1.0 / (l_o * w_o + w_a + w_b)
-        mixed = (
-            acc[g] * (w_o * inverse)
-            + oa[:, cols].astype(jnp.float32) * (w_a * inverse)
-            + ob[:, cols] * (w_b * inverse)
-        )
-        out[:, cols] = jnp.where(alive, mixed, 0.0).astype(out.dtype)
-    chunk = keep_ref.shape[0] // NL
-    for i in range(NL):
-        at = pl.ds(i * chunk, chunk)
-        keep_ref[at] = out[pl.ds(pl.multiple_of(rows[i] * chunk, chunk), chunk)]
-        give_ref[at] = out[pl.ds(pl.multiple_of(rows[NL + i] * chunk, chunk), chunk)]
+        mixed, _, _ = fold([stored(oa, ta, g, heads), stored(ob, tb, g, heads)], g, heads)
+        out[:, g * HD : (g + 1) * HD] = jnp.where(alive, mixed, 0.0).astype(out.dtype)
+    chunk = tokens // (2 * NL)
+    per = outs[0].shape[0] // chunk
+    for i, o_ref in enumerate(outs):
+        for k in range(per):
+            o_ref[k * chunk : (k + 1) * chunk] = out[pl.ds(pl.multiple_of(rows[i * per + k] * chunk, chunk), chunk)]
+
+
+def merge(rows, count, oa, sa, ob, sb):
+    tokens, width = oa.shape
+    half = jax.ShapeDtypeStruct((tokens // 2, width), jnp.bfloat16)
+    return pl.pallas_call(
+        merge_kernel,
+        out_shape=[half] * 2,
+        in_specs=[SM, SM] + [VM] * 4,
+        out_specs=[VM] * 2,
+        scratch_shapes=[pltpu.VMEM((tokens, width), jnp.bfloat16)],
+        compiler_params=SMALL,
+        cost_estimate=pl.CostEstimate(flops=8 * tokens * width, bytes_accessed=10 * tokens * width, transcendentals=0),
+    )(rows, count, oa, sa, ob, sb)
 
 
 def state_of(heads, tokens):
     return [pltpu.VMEM((heads, tokens, HD), jnp.float32)] * 3
 
 
-def causal_attention(q, k, v, out_types):
-    tokens, width = q.shape
-    return pl.pallas_call(
-        causal_kernel,
-        out_shape=out_types,
-        in_specs=[VM] * 3,
-        out_specs=[VM] * 2,
-        scratch_shapes=state_of(width // HD, tokens),
-        compiler_params=PARAMS,
-        cost_estimate=pl.CostEstimate(
-            flops=4 * tokens * width * tokens, bytes_accessed=8 * tokens * width, transcendentals=tokens * tokens * 4
-        ),
-    )(q, k, v)
-
-
-def attention(body, tab, q, kv, more, more_specs, out_types, first, more_scratch=()):
+def attention(body, tab, q, kv, more, more_specs, out_types, params):
     n, bl = tab.shape[0] - 3, kv.shape[2]
     tokens, width = q.shape
     heads = width // HD
     keys = n * bl
     return pl.pallas_call(
-        functools.partial(body, first=first),
+        body,
         out_shape=out_types,
-        in_specs=[SM, VM, ANY] + more_specs,
+        in_specs=[SM, ANY, ANY] + more_specs,
         out_specs=[VM] * len(out_types),
         scratch_shapes=[
+            pltpu.VMEM((tokens, width), jnp.bfloat16),
             pltpu.VMEM((n, 2, bl, HD), jnp.bfloat16),
             *state_of(heads, tokens),
-            pltpu.SemaphoreType.DMA((max(keys // CK, 1),)),
-            *more_scratch,
+            pltpu.SemaphoreType.DMA((max(keys // CK, 1) + 1,)),
         ],
-        compiler_params=PARAMS,
+        compiler_params=params,
         cost_estimate=pl.CostEstimate(
             flops=4 * tokens * width * keys, bytes_accessed=keys * HD * 4, transcendentals=tokens * heads * keys
         ),
     )(tab, q, kv, *more)
 
 
-def project_kernel(x_a, x_b, w_a, w_b, *outs):
-    part = jnp.dot(x_a[...], w_a[...], preferred_element_type=jnp.float32)
-    part = part + jnp.dot(x_b[...], w_b[...], preferred_element_type=jnp.float32)
-    chunk = outs[0].shape[0]
-    for i, out in enumerate(outs):
-        out[...] = part[i * chunk : (i + 1) * chunk].astype(out.dtype)
-
-
-def project(x_a, x_b, w_a, w_b, cols=512):
+def project_kernel(x_a, x_b, w_a, w_b, *refs):
+    (*outs, buf, sems) = refs
+    blocks, _, cols = buf.shape
+
+    def copy(c):
+        at = pl.ds(pl.multiple_of(c * cols, cols), cols)
+        return pltpu.make_async_copy(w_b.at[:, at], buf.at[c], sems.at[c])
+
+    def start(c, carry):
+        copy(c).start()
+        return carry
+
+    lax.fori_loop(0, blocks, start, 0)
+
+    def block(c, carry):
+        at = pl.ds(pl.multiple_of(c * cols, cols), cols)
+        part = jnp.dot(x_a[...], w_a[:, at], preferred_element_type=jnp.float32)
+        copy(c).wait()
+        part = part + jnp.dot(x_b[...], buf[c], preferred_element_type=jnp.float32)
+        chunk = part.shape[0] // len(outs)
+        for i, out in enumerate(outs):
+            out[:, at] = part[i * chunk : (i + 1) * chunk].astype(out.dtype)
+        return carry
+
+    lax.fori_loop(0, blocks, block, 0)
+
+
+def project(x_a, x_b, w_a, w_b, cols=1024):
     rows, depth = x_a.shape
     width = w_a.shape[1]
-    whole = pl.BlockSpec((rows, depth), lambda c: (0, 0))
-    tall = pl.BlockSpec((depth, cols), lambda c: (0, c))
     return pl.pallas_call(
         project_kernel,
-        grid=(width // cols,),
         out_shape=[jax.ShapeDtypeStruct((rows // NL, width), x_a.dtype)] * NL,
-        in_specs=[whole, whole, tall, tall],
-        out_specs=[pl.BlockSpec((rows // NL, cols), lambda c: (0, c))] * NL,
-        compiler_params=PARAMS,
+        in_specs=[VM, VM, VM, ANY],
+        out_specs=[VM] * NL,
+        scratch_shapes=[
+            pltpu.VMEM((width // cols, depth, cols), w_b.dtype),
+            pltpu.SemaphoreType.DMA((width // cols,)),
+        ],
+        compiler_params=SMALL,
         cost_estimate=pl.CostEstimate(
             flops=4 * rows * depth * width, bytes_accessed=4 * depth * width + 2 * rows * width, transcendentals=0
         ),
@@ -331,11 +362,15 @@
     return [(2 * a + k, 2 * b + k) for a, b in hops for k in range(2)]
 
 
-def scatter_sum(own, for_b, for_ac, for_d):
-    f32 = jnp.float32
+def scatter_start(own, for_b, for_ac, for_d):
     from_a = lax.ppermute(for_ac, "tp", along_z([(0, 1), (3, 2)]))
     from_b = lax.ppermute(for_b, "tp", along_z([(0, 2), (3, 1), (1, 0), (2, 3)]))
     from_c = lax.ppermute(for_ac, "tp", along_z([(1, 2), (2, 1)]))
+    return [own, for_d, from_a, from_b, from_c]
+
+
+def scatter_end(own, for_d, from_a, from_b, from_c):
+    f32 = jnp.float32
     for_d = (for_d.astype(f32) + from_a.astype(f32)).astype(own.dtype)
     from_d = lax.ppermute(for_d, "tp", along_z([(0, 1), (1, 3), (3, 2), (2, 0)]))
     summed = own.astype(f32) + from_b.astype(f32) + from_c.astype(f32) + from_d.astype(f32)
@@ -364,8 +399,10 @@
     t_me = lax.axis_index("tp")
     zh = (me // NY) % NZ
     flip = [(p, p ^ NY) for p in range(n_pool)]
-    cores = [(t, t ^ 1) for t in range(2 * NL)]
     planes = [[(x * NZ + z) * NY + y for x in range(NX) for y in range(NY)] for z in range(NZ)]
+
+    def swap(x, bits):
+        return lax.ppermute(x, "tp", [(t, t ^ bits) for t in range(2 * NL)])
 
     def a2a(x, groups=None):
         return lax.all_to_all(x, "pool", 0, 0, axis_index_groups=groups, tiled=True)
@@ -374,7 +411,14 @@
     ids = a2a(info)
     q_far = lax.ppermute(queries, "pool", flip)
     info_far = lax.ppermute(info, "pool", flip)
-    w_other = lax.ppermute(out_weight, "tp", cores)
+    w_core = swap(out_weight, 1)
+    info_far = lax.ppermute(info, "pool", flip)
+    w_core = swap(out_weight, 1)
+    x_y = (me // (NZ * NY)) * NY + me % NY
+    piece = out_weight.shape[0] // plane_n
+    w_piece = swap(lax.dynamic_slice_in_dim(out_weight, x_y * piece, piece, 0), 4)
+    w_piece, ids = lax.optimization_barrier((w_piece, ids))
+    w_z = lax.all_gather(w_piece, "pool", axis=0, tiled=True, axis_index_groups=planes)
 
     i = jnp.arange(plane_n, dtype=jnp.int32)
     base = (i // NY) * (NZ * NY) + i % NY
@@ -399,29 +443,22 @@
     send_b = gather_blocks(dest, ids, kv_pool, [(0, k) for k in range(per)], (near, away))
     tab_far = block_table(info_far, zh, per, (0, per), bl)
     tab = block_table(info, zh, per, (0, per), bl)
+    send_b, q_far, w_core, tab_far, tab = lax.optimization_barrier((send_b, q_far, w_core, tab_far, tab))
+    got_b = a2a(send_b, planes)
+
     st_type = jax.ShapeDtypeStruct((2 * heads, tokens), jnp.float32)
+    st_wide = jax.ShapeDtypeStruct((tokens, HD), jnp.float32)
     o_type = jax.ShapeDtypeStruct((tokens, width), jnp.bfloat16)
     o_wide = jax.ShapeDtypeStruct((tokens, width), jnp.float32)
-    o_b, st_b = causal_attention(queries, k_new, v_new, [o_wide, st_type])
-    send_b, q_far, w_other, tab_far, tab, o_b, st_b = lax.optimization_barrier(
-        (send_b, q_far, w_other, tab_far, tab, o_b, st_b)
-    )
-    got_b = a2a(send_b, planes)
-
-    o_far, st_far = attention(partner_kernel, tab_far, q_far, got_a, (), [], [o_type, st_type], 0)
-    o_a = lax.ppermute(o_far, "pool", flip)
-    st_a = lax.ppermute(st_far, "pool", flip)
+    o_a, st_a = attention(partner_kernel, tab_far, q_far, got_a, (), [], [o_type, st_type], LARGE)
+    o_a, st_a = lax.ppermute(o_a, "pool", flip), lax.ppermute(st_a, "pool", flip)
+    o_b, st_b = attention(own_kernel, tab, queries, got_b, (k_new, v_new), [VM] * 2, [o_wide, st_wide], SMALL)
 
     core, j = t_me % 2, t_me // 2
     mine = 2 * jnp.array(SENDS, jnp.int32)[j]
     rows = jnp.concatenate([mine + core, mine + 1 - core])
-    half = jax.ShapeDtypeStruct((tokens // 2, width), jnp.bfloat16)
-    x_keep, x_give = attention(
-        late_kernel, tab, queries, got_b, (o_a, st_a, o_b, st_b, rows), [VM] * 4 + [SM], [half, half], 0,
-        (pltpu.VMEM((tokens, width), jnp.bfloat16),),
-    )
-    x_got = lax.ppermute(x_give, "tp", cores)
-    summed = scatter_sum(*project(x_keep, x_got, out_weight, w_other))
+    x_keep, x_give = merge(rows, new_count, o_a, st_a, o_b, st_b)
+    summed = scatter_end(*scatter_start(*project(x_keep, swap(x_give, 1), out_weight, w_core)))
 
     arrived = got_b[:, 2 * per].reshape(NX, NY, 2, 2 * PG, HD)
     near_in, far_in = arrived[:, :, 0], arrived[:, :, 1]

time: 183 us -> 166 us (0.907)
  the two profiles are of different devices: /device:TPU:2 before, /device:TPU:28 now
where the time goes in v3:
time: 166 us; the launch traced here: 164 us
  starting transfers between devices  54.1 us (33%)
  waiting for transfers between devices  51 us (31%)
  Pallas kernels  37.2 us (22%)
  other arithmetic  10.4 us (6%)
  local copies, waits for them, and re-layouts  6.74 us (4%)
  between operations  4.78 us (3%)
    all_to_all x3, starting transfers between devices, a2a(): return lax.all_to_all(x, 'pool', 0, 0, axis_index_groups=groups, tiled=True)  23.5 us
    pallas_call x2, Pallas kernels, attention(): pl.pallas_call(body, out_shape=out_types, in_specs=[SM, ANY, ANY] + more_...  22.1 us
    all_to_all x3, waiting for transfers between devices, a2a(): return lax.all_to_all(x, 'pool', 0, 0, axis_index_groups=groups, tiled=True)  16.5 us
    ppermute x1, waiting for transfers between devices, scatter_end(): lax.ppermute(for_d, 'tp', along_z([(0, 1), (1, 3), (3, 2), (2, 0)]))  13.6 us
    ppermute x1, waiting for transfers between devices, scatter_start(): from_a = lax.ppermute(for_ac, 'tp', along_z([(0, 1), (3, 2)]))  9.42 us
    ppermute x1, starting transfers between devices, local(): lax.ppermute(o_a, 'pool', flip)  9.05 us
    pallas_call x2, Pallas kernels, gather_blocks(): pl.pallas_call(functools.partial(gather_kernel, takes=takes, paged=bool(p...  7.75 us
    ppermute x1, starting transfers between devices, local(): info_far = lax.ppermute(info, 'pool', flip)  7.19 us
  transfers between devices with their start and end apart: 14, of which 8 were waited for; matrix products, arithmetic and copies ran while one was open for 9% of the time, Pallas kernels for 19%

profile of v3, /device:TPU:28, one launch (start us, length us, event | category | flops | bytes accessed | tf_op | source)
XLA Modules:
  0.0 164.3 jit_solution(17372249956979365052)
XLA Ops:
  0.6 0.1 collective-permute-start.3
  2.0 1.6 shard_map.122
  3.6 7.2 %collective-permute-start = (s32[32,128]{1,0:T(8,128)}, s32[32,128]{1,0:T(8,128)S(1)}, u32[]{:S(2)}, u32[]{:S(2)}) collective-permute-start(s32[32,128]{1,0:T(8,128)} %shard_map.122), channel_id=1, source_target_pairs={{0,32},{8,40},{16,48},{24,56},{32,0},{40,8},{48,16},{56,24},{64,96... | collective-permute-start | bytes 49160 | tf_op jit(solution)/shard_map/ppermute | solution.py:415
  10.8 7.3 %all-to-all-start = ((s32[32,1,128]{2,1,0:T(1,128)}), s32[32,1,128]{2,1,0:T(1,128)S(1)}, u32[]{:S(2)}, u32[]{:S(2)}) async-start(s32[32,1,128]{2,1,0:T(1,128)} %bitcast.52), calls=%async_computation | async-start | bytes 32768 | tf_op jit(solution)/shard_map/all_to_all | solution.py:408
  18.0 5.5 %collective-permute-start.2 = (bf16[512,512]{1,0:T(8,128)(2,1)}, bf16[512,512]{1,0:T(8,128)(2,1)S(1)}, u32[]{:S(2)}, u32[]{:S(2)}) collective-permute-start(bf16[512,512]{1,0:T(8,128)(2,1)} %q_in.1), channel_id=1, source_target_pairs={{0,32},{8,40},{16,48},{24,56},{32,0},{40,8},{48,16},{56,24},{64,96... | collective-permute-start | bytes 1572872 | tf_op jit(solution)/shard_map/ppermute | solution.py:412
  23.6 0.5 pad_add_fusion.refs_0_
  24.1 2.5 %all-to-all-done = s32[32,1,128]{2,1,0:T(1,128)S(1)} async-done(((s32[32,1,128]{2,1,0:T(1,128)}), s32[32,1,128]{2,1,0:T(1,128)S(1)}, u32[]{:S(2)}, u32[]{:S(2)}) %all-to-all-start) | async-done | bytes 16416 | tf_op jit(solution)/shard_map/all_to_all | solution.py:408
  26.6 0.6 copy-done.5
  27.2 3.8 %shard_map.123 = bf16[16,8,64,128]{3,2,1,0:T(8,128)(2,1)} custom-call(s32[2,16]{1,0:T(2,128)} %pad_add_fusion.refs_0_, s32[32,128]{1,0:T(8,128)} %bitcast.53, bf16[192,2,64,128]{3,2,1,0:T(8,128)(2,1)} %refs_2_.3), custom_call_target="tpu_custom_call" | custom-call | bytes 4194304 | tf_op jit(solution)/shard_map/pallas_call | solution.py:99
  31.0 8.3 %all-to-all-start.1 = ((bf16[16,8,64,128]{3,2,1,0:T(8,128)(2,1)}), bf16[16,8,64,128]{3,2,1,0:T(8,128)(2,1)}, u32[]{:S(2)}, u32[]{:S(2)}) async-start(bf16[16,8,64,128]{3,2,1,0:T(8,128)(2,1)} %shard_map.123), calls=%async_computation.1 | async-start | bytes 4194304 | tf_op jit(solution)/shard_map/all_to_all | solution.py:408
  39.3 0.1 slice.28
  39.4 0.1 copy.49
  39.5 0.1 slice.31
  39.6 0.1 copy.50
  39.7 0.6 fusion.9
  40.3 0.6 fusion.8
  40.9 0.7 broadcast_compare_fusion.1
  41.6 1.3 convert_reduce_fusion.2
  42.9 0.7 broadcast_select_fusion.3
  43.6 0.1 copy.40
  43.7 0.1 eq.79
  45.1 0.1 copy.41
  45.2 0.1 reshape.230
  45.3 0.1 copy.43
  45.4 0.1 eq.83
  45.5 0.6 broadcast_select_fusion.2
  46.1 0.1 copy.44
  46.2 0.1 reshape.233
  46.3 0.1 select_reduce_fusion.2
  46.5 0.1 broadcast_select_fusion.1
  46.7 0.6 gather_fusion
  47.3 0.7 constant_dynamic-slice_fusion.2
  48.0 0.5 collective-permute-start.1
  48.5 0.1 convert_reduce_fusion.1
  48.6 0.1 convert_reduce_fusion
  48.7 0.1 select_reduce_fusion
  48.8 1.9 %pad_add_fusion.2.tab = s32[67]{0:T(128)} fusion(s32[1]{0:T(128)} %bitcast.18, s32[1]{0:T(128)} %bitcast.17, s32[1]{0:T(128)} %bitcast.16, s32[64]{0:T(128)S(1)} %get-tuple-element.51), kind=kLoop, calls=%fused_computation.58 | loop fusion | flops 201 | bytes 536 | tf_op jit(solution)/shard_map/concatenate | solution.py:69
  52.0 1.3 pad_add_fusion.3.tab
  53.3 3.8 %collective-permute-done.1.refs_4_ = bf16[16,32,128]{2,1,0:T(8,128)(2,1)S(1)} collective-permute-done((bf16[16,32,128]{2,1,0:T(8,128)(2,1)S(1)}, bf16[16,32,128]{2,1,0:T(8,128)(2,1)S(1)}, u32[]{:S(2)}, u32[]{:S(2)}) %collective-permute-start.1) | collective-permute-done | bytes 131104 | tf_op jit(solution)/shard_map/ppermute | solution.py:441
  57.1 0.7 copy-done.6
  57.7 4.0 %shard_map.124 = bf16[16,9,64,128]{3,2,1,0:T(8,128)(2,1)} custom-call(s32[2,16]{1,0:T(2,128)} %pad_add_fusion.refs_0_, s32[32,128]{1,0:T(8,128)} %bitcast.54, bf16[192,2,64,128]{3,2,1,0:T(8,128)(2,1)} %refs_2_.3, bf16[16,32,128]{2,1,0:T(8,128)(2,1)} %bitcast.48, bf16[16,32,128]{2,1,0:T(8,128)(2,1)} %copy-done.6), custom_call_target="tpu_custom_call" | custom-call | bytes 4718592 | tf_op jit(solution)/shard_map/pallas_call | solution.py:99
  61.8 3.1 %all-to-all-done.1.kv_in = bf16[16,8,64,128]{3,2,1,0:T(8,128)(2,1)} async-done(((bf16[16,8,64,128]{3,2,1,0:T(8,128)(2,1)}), bf16[16,8,64,128]{3,2,1,0:T(8,128)(2,1)}, u32[]{:S(2)}, u32[]{:S(2)}) %all-to-all-start.1) | async-done | bytes 2097184 | tf_op jit(solution)/shard_map/all_to_all | solution.py:408
  64.9 7.9 %all-to-all-start.2 = ((bf16[16,9,64,128]{3,2,1,0:T(8,128)(2,1)}), bf16[16,9,64,128]{3,2,1,0:T(8,128)(2,1)}, u32[]{:S(2)}, u32[]{:S(2)}) async-start(bf16[16,9,64,128]{3,2,1,0:T(8,128)(2,1)} %shard_map.124), calls=%async_computation.2 | async-start | bytes 4718592 | tf_op jit(solution)/shard_map/all_to_all | solution.py:408
  72.8 6.9 %shard_map.125 = (bf16[512,512]{1,0:T(8,128)(2,1)}, f32[8,512]{1,0:T(8,128)}) custom-call(s32[67]{0:T(128)} %pad_add_fusion.2.tab, bf16[512,512]{1,0:T(8,128)(2,1)} %copy-done.7, bf16[16,8,64,128]{3,2,1,0:T(8,128)(2,1)} %all-to-all-done.1.kv_in), custom_call_target="tpu_custom_call" | custom-call | flops 4294967296 | bytes 2097152 | tf_op jit(solution)/shard_map/pallas_call | solution.py:297
  79.7 9.0 %collective-permute-start.4 = (bf16[512,512]{1,0:T(8,128)(2,1)}, bf16[512,512]{1,0:T(8,128)(2,1)S(1)}, u32[]{:S(2)}, u32[]{:S(2)}) collective-permute-start(bf16[512,512]{1,0:T(8,128)(2,1)} %get-tuple-element.31), channel_id=1, source_target_pairs={{0,32},{8,40},{16,48},{24,56},{32,0},{40,8},{48,16},{56,24},{64,96... | collective-permute-start | bytes 1572872 | tf_op jit(solution)/shard_map/ppermute | solution.py:454
  88.8 0.7 add_bitcast_fusion
  89.5 0.1 pad_add_fusion.1.rows
  89.6 10.9 %all-to-all-done.2.kv_in = bf16[16,9,64,128]{3,2,1,0:T(8,128)(2,1)} async-done(((bf16[16,9,64,128]{3,2,1,0:T(8,128)(2,1)}), bf16[16,9,64,128]{3,2,1,0:T(8,128)(2,1)}, u32[]{:S(2)}, u32[]{:S(2)}) %all-to-all-start.2) | async-done | bytes 2359328 | tf_op jit(solution)/shard_map/all_to_all | solution.py:408
  100.5 15.3 %shard_map.126 = (f32[512,512]{1,0:T(8,128)S(1)}, f32[512,128]{1,0:T(8,128)S(1)}) custom-call(s32[67]{0:T(128)S(1)} %pad_add_fusion.3.tab, bf16[512,512]{1,0:T(8,128)(2,1)S(1)} %copy-done.3, bf16[16,9,64,128]{3,2,1,0:T(8,128)(2,1)} %all-to-all-done.2.kv_in, bf16[512,128]{1,0:T(8,128)(2,1)S(1)} %copy-done.1, bf16[512,128]{1,0:T(8,128)(2,1)S(1)} %copy-done.2), custom_call_target="tpu_custom_call" | custom-call | flops 4294967296 | bytes 2097152 | tf_op jit(solution)/shard_map/pallas_call | solution.py:297
  115.7 1.5 shard_map.127
  117.2 0.1 collective-permute-start.6
  117.3 1.5 collective-permute-done.6.x_b
  118.8 4.3 %shard_map.128 = (bf16[64,4096]{1,0:T(8,128)(2,1)S(1)}, bf16[64,4096]{1,0:T(8,128)(2,1)S(1)}, bf16[64,4096]{1,0:T(8,128)(2,1)S(1)}, bf16[64,4096]{1,0:T(8,128)(2,1)S(1)}) custom-call(bf16[256,512]{1,0:T(8,128)(2,1)S(1)} %get-tuple-element.37.x_a, bf16[256,512]{1,0:T(8,128)(2,1)S(1)} %collective-permute-done.6.x_b, bf16[512,4096]{1,0:T(8,128)(2,1)S(1)} %copy-done, ...), custom_call_target="tpu_custom_call" | custom-call | flops 2147483648 | bytes 10485760 | tf_op jit(solution)/shard_map/pallas_call | solution.py:345
  123.2 2.9 %collective-permute-start.9 = (bf16[64,4096]{1,0:T(8,128)(2,1)S(1)}, bf16[64,4096]{1,0:T(8,128)(2,1)S(1)}, u32[]{:S(2)}, u32[]{:S(2)}) collective-permute-start(bf16[64,4096]{1,0:T(8,128)(2,1)S(1)} %get-tuple-element.42), channel_id=1, source_target_pairs={{0,2},{1,3},{6,4},{7,5},{8,10},{9,11},{14,12},{15,13},{16,18},{17,... | collective-permute-start | bytes 1572872 | tf_op jit(solution)/shard_map/ppermute | solution.py:366
  126.1 0.7 collective-permute-start.8
  126.8 2.1 %collective-permute-start.7 = (bf16[64,4096]{1,0:T(8,128)(2,1)S(1)}, bf16[64,4096]{1,0:T(8,128)(2,1)S(1)}, u32[]{:S(2)}, u32[]{:S(2)}) collective-permute-start(bf16[64,4096]{1,0:T(8,128)(2,1)S(1)} %get-tuple-element.41), channel_id=1, source_target_pairs={{0,4},{1,5},{6,2},{7,3},{2,0},{3,1},{4,6},{5,7},{8,12},{9,13},{14,... | collective-permute-start | bytes 1572872 | tf_op jit(solution)/shard_map/ppermute | solution.py:367
  128.9 9.4 %collective-permute-done.9 = bf16[64,4096]{1,0:T(8,128)(2,1)S(1)} collective-permute-done((bf16[64,4096]{1,0:T(8,128)(2,1)S(1)}, bf16[64,4096]{1,0:T(8,128)(2,1)S(1)}, u32[]{:S(2)}, u32[]{:S(2)}) %collective-permute-start.9) | collective-permute-done | bytes 524320 | tf_op jit(solution)/shard_map/ppermute | solution.py:366
  138.3 0.9 add_convert_fusion.1
  139.2 2.5 %collective-permute-start.10 = (bf16[64,4096]{1,0:T(8,128)(2,1)}, bf16[64,4096]{1,0:T(8,128)(2,1)S(1)}, u32[]{:S(2)}, u32[]{:S(2)}) collective-permute-start(bf16[64,4096]{1,0:T(8,128)(2,1)} %add_convert_fusion.1), channel_id=1, source_target_pairs={{0,2},{1,3},{2,6},{3,7},{6,4},{7,5},{4,0},{5,1},{8,10},{9,11},{10,... | collective-permute-start | bytes 1572872 | tf_op jit(solution)/shard_map/ppermute | solution.py:375
  141.7 1.0 slice.38
  142.8 0.7 copy.46
  143.5 6.1 %collective-permute-done.7 = bf16[64,4096]{1,0:T(8,128)(2,1)S(1)} collective-permute-done((bf16[64,4096]{1,0:T(8,128)(2,1)S(1)}, bf16[64,4096]{1,0:T(8,128)(2,1)S(1)}, u32[]{:S(2)}, u32[]{:S(2)}) %collective-permute-start.7) | collective-permute-done | bytes 524320 | tf_op jit(solution)/shard_map/ppermute | solution.py:367
  149.6 13.6 %collective-permute-done.10 = bf16[64,4096]{1,0:T(8,128)(2,1)S(1)} collective-permute-done((bf16[64,4096]{1,0:T(8,128)(2,1)}, bf16[64,4096]{1,0:T(8,128)(2,1)S(1)}, u32[]{:S(2)}, u32[]{:S(2)}) %collective-permute-start.10) | collective-permute-done | bytes 524320 | tf_op jit(solution)/shard_map/ppermute | solution.py:375
  163.2 1.1 add_convert_fusion
  (37 shorter events, 0.3 us)
Async XLA Ops:
  0.6 61.1 %collective-permute-start.3 = (bf16[512,4096]{1,0:T(8,128)(2,1)}, bf16[512,4096]{1,0:T(8,128)(2,1)}, u32[]{:S(2)}, u32[]{:S(2)}) collective-permute-start(bf16[512,4096]{1,0:T(8,128)(2,1)} %w_a.1), channel_id=1, source_target_pairs={{0,1},{1,0},{2,3},{3,2},{4,5},{5,4},{6,7},{7,6},{8,9},{9,8},{10,11... | collective-permute-start | bytes 12582920 | tf_op jit(solution)/shard_map/ppermute | solution.py:405
  3.6 35.7 %collective-permute-start = (s32[32,128]{1,0:T(8,128)}, s32[32,128]{1,0:T(8,128)S(1)}, u32[]{:S(2)}, u32[]{:S(2)}) collective-permute-start(s32[32,128]{1,0:T(8,128)} %shard_map.122), channel_id=1, source_target_pairs={{0,32},{8,40},{16,48},{24,56},{32,0},{40,8},{48,16},{56,24},{64,96... | collective-permute-start | bytes 49160 | tf_op jit(solution)/shard_map/ppermute | solution.py:415
  10.8 15.8 %all-to-all-start = ((s32[32,1,128]{2,1,0:T(1,128)}), s32[32,1,128]{2,1,0:T(1,128)S(1)}, u32[]{:S(2)}, u32[]{:S(2)}) async-start(s32[32,1,128]{2,1,0:T(1,128)} %bitcast.52), calls=%async_computation | async-start | bytes 32768 | tf_op jit(solution)/shard_map/all_to_all | solution.py:408
  18.0 43.7 %collective-permute-start.2 = (bf16[512,512]{1,0:T(8,128)(2,1)}, bf16[512,512]{1,0:T(8,128)(2,1)S(1)}, u32[]{:S(2)}, u32[]{:S(2)}) collective-permute-start(bf16[512,512]{1,0:T(8,128)(2,1)} %q_in.1), channel_id=1, source_target_pairs={{0,32},{8,40},{16,48},{24,56},{32,0},{40,8},{48,16},{56,24},{64,96... | collective-permute-start | bytes 1572872 | tf_op jit(solution)/shard_map/ppermute | solution.py:412
  26.6 0.6 copy-start.5
  31.0 8.5 %copy-start.4 = (s32[32,128]{1,0:T(8,128)S(1)}, s32[32,128]{1,0:T(8,128)}, u32[]{:S(2)}) copy-start(s32[32,128]{1,0:T(8,128)} %shard_map.122) | copy-start | bytes 49156
  31.0 15.4 %copy-start.8 = (s32[1,32]{1,0:T(1,128)S(1)}, s32[1,32]{1,0:T(1,128)}, u32[]{:S(2)}) copy-start(s32[1,32]{1,0:T(1,128)} %param.20) | copy-start | bytes 388
  31.0 15.5 %copy-start.1 = (bf16[512,128]{1,0:T(8,128)(2,1)S(1)}, bf16[512,128]{1,0:T(8,128)(2,1)}, u32[]{:S(2)}) copy-start(bf16[512,128]{1,0:T(8,128)(2,1)} %k_ref) | copy-start | bytes 393220
  31.0 15.5 %copy-start.2 = (bf16[512,128]{1,0:T(8,128)(2,1)S(1)}, bf16[512,128]{1,0:T(8,128)(2,1)}, u32[]{:S(2)}) copy-start(bf16[512,128]{1,0:T(8,128)(2,1)} %v_ref) | copy-start | bytes 393220
  31.0 33.9 %all-to-all-start.1 = ((bf16[16,8,64,128]{3,2,1,0:T(8,128)(2,1)}), bf16[16,8,64,128]{3,2,1,0:T(8,128)(2,1)}, u32[]{:S(2)}, u32[]{:S(2)}) async-start(bf16[16,8,64,128]{3,2,1,0:T(8,128)(2,1)} %shard_map.123), calls=%async_computation.1 | async-start | bytes 4194304 | tf_op jit(solution)/shard_map/all_to_all | solution.py:408
  48.0 9.1 %collective-permute-start.1 = (bf16[16,32,128]{2,1,0:T(8,128)(2,1)S(1)}, bf16[16,32,128]{2,1,0:T(8,128)(2,1)S(1)}, u32[]{:S(2)}, u32[]{:S(2)}) collective-permute-start(bf16[16,32,128]{2,1,0:T(8,128)(2,1)S(1)} %bitcast.55), channel_id=1, source_target_pairs={{0,32},{8,40},{16,48},{24,56},{32,0},{40,8},{48,16},{56,24},{64,96... | collective-permute-start | bytes 393224 | tf_op jit(solution)/shard_map/ppermute | solution.py:441
  57.1 0.7 copy-start.6
  61.7 3.2 %copy-start.7 = (bf16[512,512]{1,0:T(8,128)(2,1)}, bf16[512,512]{1,0:T(8,128)(2,1)S(1)}, u32[]{:S(2)}) copy-start(bf16[512,512]{1,0:T(8,128)(2,1)S(1)} %collective-permute-done.2.q_in) | copy-start | bytes 1572868
  64.9 35.6 %all-to-all-start.2 = ((bf16[16,9,64,128]{3,2,1,0:T(8,128)(2,1)}), bf16[16,9,64,128]{3,2,1,0:T(8,128)(2,1)}, u32[]{:S(2)}, u32[]{:S(2)}) async-start(bf16[16,9,64,128]{3,2,1,0:T(8,128)(2,1)} %shard_map.124), calls=%async_computation.2 | async-start | bytes 4718592 | tf_op jit(solution)/shard_map/all_to_all | solution.py:408
  72.8 27.6 %copy-start.3 = (bf16[512,512]{1,0:T(8,128)(2,1)S(1)}, bf16[512,512]{1,0:T(8,128)(2,1)}, u32[]{:S(2)}) copy-start(bf16[512,512]{1,0:T(8,128)(2,1)} %q_in.1) | copy-start | bytes 1572868
  79.7 36.0 %collective-permute-start.4 = (bf16[512,512]{1,0:T(8,128)(2,1)}, bf16[512,512]{1,0:T(8,128)(2,1)S(1)}, u32[]{:S(2)}, u32[]{:S(2)}) collective-permute-start(bf16[512,512]{1,0:T(8,128)(2,1)} %get-tuple-element.31), channel_id=1, source_target_pairs={{0,32},{8,40},{16,48},{24,56},{32,0},{40,8},{48,16},{56,24},{64,96... | collective-permute-start | bytes 1572872 | tf_op jit(solution)/shard_map/ppermute | solution.py:454
  89.5 26.2 %collective-permute-start.5 = (f32[8,512]{1,0:T(8,128)}, f32[8,512]{1,0:T(8,128)S(1)}, u32[]{:S(2)}, u32[]{:S(2)}) collective-permute-start(f32[8,512]{1,0:T(8,128)} %get-tuple-element.32), channel_id=1, source_target_pairs={{0,32},{8,40},{16,48},{24,56},{32,0},{40,8},{48,16},{56,24},{64,96... | collective-permute-start | bytes 49160 | tf_op jit(solution)/shard_map/ppermute | solution.py:454
  100.5 18.4 %copy-start = (bf16[512,4096]{1,0:T(8,128)(2,1)S(1)}, bf16[512,4096]{1,0:T(8,128)(2,1)}, u32[]{:S(2)}) copy-start(bf16[512,4096]{1,0:T(8,128)(2,1)} %w_a.1) | copy-start | bytes 12582916
  117.2 1.6 collective-permute-start.6
  123.2 15.1 %collective-permute-start.9 = (bf16[64,4096]{1,0:T(8,128)(2,1)S(1)}, bf16[64,4096]{1,0:T(8,128)(2,1)S(1)}, u32[]{:S(2)}, u32[]{:S(2)}) collective-permute-start(bf16[64,4096]{1,0:T(8,128)(2,1)S(1)} %get-tuple-element.42), channel_id=1, source_target_pairs={{0,2},{1,3},{6,4},{7,5},{8,10},{9,11},{14,12},{15,13},{16,18},{17,... | collective-permute-start | bytes 1572872 | tf_op jit(solution)/shard_map/ppermute | solution.py:366
  126.1 23.5 %collective-permute-start.8 = (bf16[64,4096]{1,0:T(8,128)(2,1)S(1)}, bf16[64,4096]{1,0:T(8,128)(2,1)S(1)}, u32[]{:S(2)}, u32[]{:S(2)}) collective-permute-start(bf16[64,4096]{1,0:T(8,128)(2,1)S(1)} %get-tuple-element.42), channel_id=1, source_target_pairs={{2,4},{3,5},{4,2},{5,3},{10,12},{11,13},{12,10},{13,11},{18,20},{1... | collective-permute-start | bytes 1572872 | tf_op jit(solution)/shard_map/ppermute | solution.py:368
  126.8 22.8 %collective-permute-start.7 = (bf16[64,4096]{1,0:T(8,128)(2,1)S(1)}, bf16[64,4096]{1,0:T(8,128)(2,1)S(1)}, u32[]{:S(2)}, u32[]{:S(2)}) collective-permute-start(bf16[64,4096]{1,0:T(8,128)(2,1)S(1)} %get-tuple-element.41), channel_id=1, source_target_pairs={{0,4},{1,5},{6,2},{7,3},{2,0},{3,1},{4,6},{5,7},{8,12},{9,13},{14,... | collective-permute-start | bytes 1572872 | tf_op jit(solution)/shard_map/ppermute | solution.py:367
  139.2 24.0 %collective-permute-start.10 = (bf16[64,4096]{1,0:T(8,128)(2,1)}, bf16[64,4096]{1,0:T(8,128)(2,1)S(1)}, u32[]{:S(2)}, u32[]{:S(2)}) collective-permute-start(bf16[64,4096]{1,0:T(8,128)(2,1)} %add_convert_fusion.1), channel_id=1, source_target_pairs={{0,2},{1,3},{2,6},{3,7},{6,4},{7,5},{4,0},{5,1},{8,10},{9,11},{10,... | collective-permute-start | bytes 1572872 | tf_op jit(solution)/shard_map/ppermute | solution.py:375

commit v4 on v3

--- a/solution.py
+++ b/solution.py
@@ -11,7 +11,7 @@
 PG = 16
 NX, NZ, NY = 4, 2, 4
 NL = 4
-SENDS = ((0, 2, 3, 1), (1, 0, 2, 3), (2, 3, 1, 0), (3, 1, 0, 2))
+SENDS = ((2, 3, 0, 1), (0, 2, 1, 3), (3, 1, 2, 0), (1, 0, 3, 2))
 CK = 1024
 NEG = -1e30
 RATE = HD ** (-0.5) * 1.4426950408889634
@@ -312,7 +312,7 @@
     )(tab, q, kv, *more)
 
 
-def project_kernel(x_a, x_b, w_a, w_b, *refs):
+def project_kernel(x_a, x_b, w_a, w_b, *refs, first):
     (*outs, buf, sems) = refs
     blocks, _, cols = buf.shape
 
@@ -325,12 +325,13 @@
         return carry
 
     lax.fori_loop(0, blocks, start, 0)
+    rows = pl.ds(first, len(outs) * outs[0].shape[0])
 
     def block(c, carry):
         at = pl.ds(pl.multiple_of(c * cols, cols), cols)
-        part = jnp.dot(x_a[...], w_a[:, at], preferred_element_type=jnp.float32)
+        part = jnp.dot(x_a[rows], w_a[:, at], preferred_element_type=jnp.float32)
         copy(c).wait()
-        part = part + jnp.dot(x_b[...], buf[c], preferred_element_type=jnp.float32)
+        part = part + jnp.dot(x_b[rows], buf[c], preferred_element_type=jnp.float32)
         chunk = part.shape[0] // len(outs)
         for i, out in enumerate(outs):
             out[:, at] = part[i * chunk : (i + 1) * chunk].astype(out.dtype)
@@ -339,21 +340,21 @@
     lax.fori_loop(0, blocks, block, 0)
 
 
-def project(x_a, x_b, w_a, w_b, cols=1024):
+def project(x_a, x_b, w_a, w_b, half, cols=1024):
     rows, depth = x_a.shape
     width = w_a.shape[1]
     return pl.pallas_call(
-        project_kernel,
-        out_shape=[jax.ShapeDtypeStruct((rows // NL, width), x_a.dtype)] * NL,
+        functools.partial(project_kernel, first=half * (rows // 2)),
+        out_shape=[jax.ShapeDtypeStruct((rows // NL, width), x_a.dtype)] * (NL // 2),
         in_specs=[VM, VM, VM, ANY],
-        out_specs=[VM] * NL,
+        out_specs=[VM] * (NL // 2),
         scratch_shapes=[
             pltpu.VMEM((width // cols, depth, cols), w_b.dtype),
             pltpu.SemaphoreType.DMA((width // cols,)),
         ],
         compiler_params=SMALL,
         cost_estimate=pl.CostEstimate(
-            flops=4 * rows * depth * width, bytes_accessed=4 * depth * width + 2 * rows * width, transcendentals=0
+            flops=2 * rows * depth * width, bytes_accessed=4 * depth * width + 2 * rows * width, transcendentals=0
         ),
     )(x_a, x_b, w_a, w_b)
 
@@ -458,7 +459,10 @@
     mine = 2 * jnp.array(SENDS, jnp.int32)[j]
     rows = jnp.concatenate([mine + core, mine + 1 - core])
     x_keep, x_give = merge(rows, new_count, o_a, st_a, o_b, st_b)
-    summed = scatter_end(*scatter_start(*project(x_keep, swap(x_give, 1), out_weight, w_core)))
+    x = (x_keep, swap(x_give, 1), out_weight, w_core)
+    for_b, for_ac = project(*x, 0)
+    own, for_d = project(*x, 1)
+    summed = scatter_end(*scatter_start(own, for_b, for_ac, for_d))
 
     arrived = got_b[:, 2 * per].reshape(NX, NY, 2, 2 * PG, HD)
     near_in, far_in = arrived[:, :, 0], arrived[:, :, 1]

time: 166 us -> 165 us (level)
  Pallas kernels: 37.2 us -> 45 us
  waiting for transfers between devices: 51 us -> 44.8 us
  starting transfers between devices: 54.1 us -> 51.2 us
    pallas_call x2, Pallas kernels: 22.1 us -> 27.5 us  [attention(): pl.pallas_call(body, out_shape=out_types, in_specs=[SM, ANY, ANY] + more_...]
    ppermute x1, starting transfers between devices: 9.05 us -> 3.72 us  [local(): lax.ppermute(o_a, 'pool', flip)]
    ppermute x1, waiting for transfers between devices: 9.42 us -> 6.12 us  [scatter_start(): from_a = lax.ppermute(for_ac, 'tp', along_z([(0, 1), (3, 2)]))]
    all_to_all x3, waiting for transfers between devices: 16.5 us -> 13.7 us  [a2a(): return lax.all_to_all(x, 'pool', 0, 0, axis_index_groups=groups, tiled=True)]
    ppermute x1, starting transfers between devices: 0.04 us -> 2.5 us  [local(): lax.ppermute(st_a, 'pool', flip)]
    pallas_call x1 -> x2, Pallas kernels: 4.34 us -> 6.61 us  [project(): pl.pallas_call(functools.partial(project_kernel, first=half * (rows // 2)...]
  transfers between devices with their start and end apart: 14 -> 14, of which waited for: 8 -> 8; matrix products, arithmetic and copies ran while one was open for 9% -> 9% of each run, Pallas kernels for 19% -> 25%
where the time goes in v4:
time: 165 us; the launch traced here: 163 us
  starting transfers between devices  51.2 us (31%)
  Pallas kernels  45 us (27%)
  waiting for transfers between devices  44.8 us (27%)
  other arithmetic  10.6 us (6%)
  local copies, waits for them, and re-layouts  6.74 us (4%)
  between operations  4.74 us (3%)
    pallas_call x2, Pallas kernels, attention(): pl.pallas_call(body, out_shape=out_types, in_specs=[SM, ANY, ANY] + more_...  27.5 us
    all_to_all x3, starting transfers between devices, a2a(): return lax.all_to_all(x, 'pool', 0, 0, axis_index_groups=groups, tiled=True)  23.4 us
    all_to_all x3, waiting for transfers between devices, a2a(): return lax.all_to_all(x, 'pool', 0, 0, axis_index_groups=groups, tiled=True)  13.7 us
    ppermute x1, waiting for transfers between devices, scatter_end(): lax.ppermute(for_d, 'tp', along_z([(0, 1), (1, 3), (3, 2), (2, 0)]))  13.6 us
    pallas_call x2, Pallas kernels, gather_blocks(): pl.pallas_call(functools.partial(gather_kernel, takes=takes, paged=bool(p...  7.78 us
    ppermute x1, starting transfers between devices, local(): info_far = lax.ppermute(info, 'pool', flip)  7.19 us
    pallas_call x2, Pallas kernels, project(): pl.pallas_call(functools.partial(project_kernel, first=half * (rows // 2)...  6.61 us
    ppermute x1, waiting for transfers between devices, scatter_start(): lax.ppermute(for_b, 'tp', along_z([(0, 2), (3, 1), (1, 0), (2, 3)]))  6.13 us
  transfers between devices with their start and end apart: 14, of which 8 were waited for; matrix products, arithmetic and copies ran while one was open for 9% of the time, Pallas kernels for 25%

profile of v4, /device:TPU:28, one launch (start us, length us, event | category | flops | bytes accessed | tf_op | source)
XLA Modules:
  0.0 163.2 jit_solution(4271430826972336789)
XLA Ops:
  0.6 0.1 collective-permute-start.3
  2.0 1.6 shard_map.122
  3.6 7.2 %collective-permute-start = (s32[32,128]{1,0:T(8,128)}, s32[32,128]{1,0:T(8,128)S(1)}, u32[]{:S(2)}, u32[]{:S(2)}) collective-permute-start(s32[32,128]{1,0:T(8,128)} %shard_map.122), channel_id=1, source_target_pairs={{0,32},{8,40},{16,48},{24,56},{32,0},{40,8},{48,16},{56,24},{64,96... | collective-permute-start | bytes 49160 | tf_op jit(solution)/shard_map/ppermute | solution.py:416
  10.8 7.3 %all-to-all-start = ((s32[32,1,128]{2,1,0:T(1,128)}), s32[32,1,128]{2,1,0:T(1,128)S(1)}, u32[]{:S(2)}, u32[]{:S(2)}) async-start(s32[32,1,128]{2,1,0:T(1,128)} %bitcast.52), calls=%async_computation | async-start | bytes 32768 | tf_op jit(solution)/shard_map/all_to_all | solution.py:409
  18.0 5.5 %collective-permute-start.2 = (bf16[512,512]{1,0:T(8,128)(2,1)}, bf16[512,512]{1,0:T(8,128)(2,1)S(1)}, u32[]{:S(2)}, u32[]{:S(2)}) collective-permute-start(bf16[512,512]{1,0:T(8,128)(2,1)} %q_in.1), channel_id=1, source_target_pairs={{0,32},{8,40},{16,48},{24,56},{32,0},{40,8},{48,16},{56,24},{64,96... | collective-permute-start | bytes 1572872 | tf_op jit(solution)/shard_map/ppermute | solution.py:413
  23.6 0.6 pad_add_fusion.refs_0_
  24.2 2.4 %all-to-all-done = s32[32,1,128]{2,1,0:T(1,128)S(1)} async-done(((s32[32,1,128]{2,1,0:T(1,128)}), s32[32,1,128]{2,1,0:T(1,128)S(1)}, u32[]{:S(2)}, u32[]{:S(2)}) %all-to-all-start) | async-done | bytes 16416 | tf_op jit(solution)/shard_map/all_to_all | solution.py:409
  26.6 0.6 copy-done.5
  27.2 3.8 %shard_map.123 = bf16[16,8,64,128]{3,2,1,0:T(8,128)(2,1)} custom-call(s32[2,16]{1,0:T(2,128)} %pad_add_fusion.refs_0_, s32[32,128]{1,0:T(8,128)} %bitcast.53, bf16[192,2,64,128]{3,2,1,0:T(8,128)(2,1)} %refs_2_.3), custom_call_target="tpu_custom_call" | custom-call | bytes 4194304 | tf_op jit(solution)/shard_map/pallas_call | solution.py:99
  31.0 8.2 %all-to-all-start.1 = ((bf16[16,8,64,128]{3,2,1,0:T(8,128)(2,1)}), bf16[16,8,64,128]{3,2,1,0:T(8,128)(2,1)}, u32[]{:S(2)}, u32[]{:S(2)}) async-start(bf16[16,8,64,128]{3,2,1,0:T(8,128)(2,1)} %shard_map.123), calls=%async_computation.1 | async-start | bytes 4194304 | tf_op jit(solution)/shard_map/all_to_all | solution.py:409
  39.3 0.1 copy.49
  39.5 0.1 copy.50
  39.6 0.6 fusion.9
  40.2 0.6 fusion.8
  40.8 0.7 broadcast_compare_fusion.1
  41.5 1.4 convert_reduce_fusion.2
  42.9 0.7 broadcast_select_fusion.3
  43.6 0.1 copy.40
  43.7 0.1 eq.79
  45.0 0.1 copy.41
  45.2 0.1 reshape.230
  45.3 0.1 copy.43
  45.4 0.1 eq.83
  45.5 0.7 broadcast_select_fusion.2
  46.2 0.1 copy.44
  46.3 0.1 reshape.233
  46.4 0.1 select_reduce_fusion.2
  46.5 0.1 broadcast_select_fusion.1
  46.7 0.6 gather_fusion
  47.3 0.7 constant_dynamic-slice_fusion.2
  48.0 0.6 collective-permute-start.1
  48.6 0.1 convert_reduce_fusion.1
  48.7 0.1 convert_reduce_fusion
  48.8 0.1 select_reduce_fusion
  48.9 1.9 %pad_add_fusion.2.tab = s32[67]{0:T(128)} fusion(s32[1]{0:T(128)} %bitcast.18, s32[1]{0:T(128)} %bitcast.17, s32[1]{0:T(128)} %bitcast.16, s32[64]{0:T(128)S(1)} %get-tuple-element.51), kind=kLoop, calls=%fused_computation.58 | loop fusion | flops 201 | bytes 536 | tf_op jit(solution)/shard_map/concatenate | solution.py:69
  52.0 1.4 pad_add_fusion.3.tab
  53.4 3.8 %collective-permute-done.1.refs_4_ = bf16[16,32,128]{2,1,0:T(8,128)(2,1)S(1)} collective-permute-done((bf16[16,32,128]{2,1,0:T(8,128)(2,1)S(1)}, bf16[16,32,128]{2,1,0:T(8,128)(2,1)S(1)}, u32[]{:S(2)}, u32[]{:S(2)}) %collective-permute-start.1) | collective-permute-done | bytes 131104 | tf_op jit(solution)/shard_map/ppermute | solution.py:442
  57.2 0.7 copy-done.6
  57.8 4.0 %shard_map.124 = bf16[16,9,64,128]{3,2,1,0:T(8,128)(2,1)} custom-call(s32[2,16]{1,0:T(2,128)} %pad_add_fusion.refs_0_, s32[32,128]{1,0:T(8,128)} %bitcast.54, bf16[192,2,64,128]{3,2,1,0:T(8,128)(2,1)} %refs_2_.3, bf16[16,32,128]{2,1,0:T(8,128)(2,1)} %bitcast.48, bf16[16,32,128]{2,1,0:T(8,128)(2,1)} %copy-done.6), custom_call_target="tpu_custom_call" | custom-call | bytes 4718592 | tf_op jit(solution)/shard_map/pallas_call | solution.py:99
  61.8 3.0 %all-to-all-done.1.kv_in = bf16[16,8,64,128]{3,2,1,0:T(8,128)(2,1)} async-done(((bf16[16,8,64,128]{3,2,1,0:T(8,128)(2,1)}), bf16[16,8,64,128]{3,2,1,0:T(8,128)(2,1)}, u32[]{:S(2)}, u32[]{:S(2)}) %all-to-all-start.1) | async-done | bytes 2097184 | tf_op jit(solution)/shard_map/all_to_all | solution.py:409
  64.8 7.9 %all-to-all-start.2 = ((bf16[16,9,64,128]{3,2,1,0:T(8,128)(2,1)}), bf16[16,9,64,128]{3,2,1,0:T(8,128)(2,1)}, u32[]{:S(2)}, u32[]{:S(2)}) async-start(bf16[16,9,64,128]{3,2,1,0:T(8,128)(2,1)} %shard_map.124), calls=%async_computation.2 | async-start | bytes 4718592 | tf_op jit(solution)/shard_map/all_to_all | solution.py:409
  72.8 12.3 %shard_map.125 = (bf16[512,512]{1,0:T(8,128)(2,1)}, f32[8,512]{1,0:T(8,128)}) custom-call(s32[67]{0:T(128)} %pad_add_fusion.2.tab, bf16[512,512]{1,0:T(8,128)(2,1)} %copy-done.7, bf16[16,8,64,128]{3,2,1,0:T(8,128)(2,1)} %all-to-all-done.1.kv_in), custom_call_target="tpu_custom_call" | custom-call | flops 4294967296 | bytes 2097152 | tf_op jit(solution)/shard_map/pallas_call | solution.py:297
  85.1 3.7 %collective-permute-start.4 = (bf16[512,512]{1,0:T(8,128)(2,1)}, bf16[512,512]{1,0:T(8,128)(2,1)S(1)}, u32[]{:S(2)}, u32[]{:S(2)}) collective-permute-start(bf16[512,512]{1,0:T(8,128)(2,1)} %get-tuple-element.31), channel_id=1, source_target_pairs={{0,32},{8,40},{16,48},{24,56},{32,0},{40,8},{48,16},{56,24},{64,96... | collective-permute-start | bytes 1572872 | tf_op jit(solution)/shard_map/ppermute | solution.py:455
  88.8 0.7 add_bitcast_fusion
  89.5 0.1 pad_add_fusion.1.rows
  89.5 2.5 %collective-permute-start.5 = (f32[8,512]{1,0:T(8,128)}, f32[8,512]{1,0:T(8,128)S(1)}, u32[]{:S(2)}, u32[]{:S(2)}) collective-permute-start(f32[8,512]{1,0:T(8,128)} %get-tuple-element.32), channel_id=1, source_target_pairs={{0,32},{8,40},{16,48},{24,56},{32,0},{40,8},{48,16},{56,24},{64,96... | collective-permute-start | bytes 49160 | tf_op jit(solution)/shard_map/ppermute | solution.py:455
  92.0 8.3 %all-to-all-done.2.kv_in = bf16[16,9,64,128]{3,2,1,0:T(8,128)(2,1)} async-done(((bf16[16,9,64,128]{3,2,1,0:T(8,128)(2,1)}), bf16[16,9,64,128]{3,2,1,0:T(8,128)(2,1)}, u32[]{:S(2)}, u32[]{:S(2)}) %all-to-all-start.2) | async-done | bytes 2359328 | tf_op jit(solution)/shard_map/all_to_all | solution.py:409
  100.4 15.3 %shard_map.126 = (f32[512,512]{1,0:T(8,128)S(1)}, f32[512,128]{1,0:T(8,128)S(1)}) custom-call(s32[67]{0:T(128)S(1)} %pad_add_fusion.3.tab, bf16[512,512]{1,0:T(8,128)(2,1)S(1)} %copy-done.3, bf16[16,9,64,128]{3,2,1,0:T(8,128)(2,1)} %all-to-all-done.2.kv_in, bf16[512,128]{1,0:T(8,128)(2,1)S(1)} %copy-done.1, bf16[512,128]{1,0:T(8,128)(2,1)S(1)} %copy-done.2), custom_call_target="tpu_custom_call" | custom-call | flops 4294967296 | bytes 2097152 | tf_op jit(solution)/shard_map/pallas_call | solution.py:297
  115.7 1.5 shard_map.127
  117.1 0.1 collective-permute-start.6
  117.2 1.5 collective-permute-done.6.x_b
  118.8 3.3 %shard_map.129 = (bf16[64,4096]{1,0:T(8,128)(2,1)S(1)}, bf16[64,4096]{1,0:T(8,128)(2,1)S(1)}) custom-call(bf16[256,512]{1,0:T(8,128)(2,1)S(1)} %get-tuple-element.37.x_a, bf16[256,512]{1,0:T(8,128)(2,1)S(1)} %collective-permute-done.6.x_b, bf16[512,4096]{1,0:T(8,128)(2,1)S(1)} %copy-done, bf16[512,4096]{1,0:T(8,128)(2,1)} %collective-permute-done.3.w_b), custom_call_target="tpu_custom_call" | custom-call | flops 1073741824 | bytes 10485760 | tf_op jit(solution)/shard_map/pallas_call | solution.py:346
  122.1 2.9 %collective-permute-start.9 = (bf16[64,4096]{1,0:T(8,128)(2,1)S(1)}, bf16[64,4096]{1,0:T(8,128)(2,1)S(1)}, u32[]{:S(2)}, u32[]{:S(2)}) collective-permute-start(bf16[64,4096]{1,0:T(8,128)(2,1)S(1)} %get-tuple-element.42), channel_id=1, source_target_pairs={{0,2},{1,3},{6,4},{7,5},{8,10},{9,11},{14,12},{15,13},{16,18},{17,... | collective-permute-start | bytes 1572872 | tf_op jit(solution)/shard_map/ppermute | solution.py:367
  125.0 0.7 collective-permute-start.8
  125.7 2.1 %collective-permute-start.7 = (bf16[64,4096]{1,0:T(8,128)(2,1)S(1)}, bf16[64,4096]{1,0:T(8,128)(2,1)S(1)}, u32[]{:S(2)}, u32[]{:S(2)}) collective-permute-start(bf16[64,4096]{1,0:T(8,128)(2,1)S(1)} %get-tuple-element.41), channel_id=1, source_target_pairs={{0,4},{1,5},{6,2},{7,3},{2,0},{3,1},{4,6},{5,7},{8,12},{9,13},{14,... | collective-permute-start | bytes 1572872 | tf_op jit(solution)/shard_map/ppermute | solution.py:368
  127.8 3.3 %shard_map.128 = (bf16[64,4096]{1,0:T(8,128)(2,1)S(1)}, bf16[64,4096]{1,0:T(8,128)(2,1)S(1)}) custom-call(bf16[256,512]{1,0:T(8,128)(2,1)S(1)} %get-tuple-element.37.x_a, bf16[256,512]{1,0:T(8,128)(2,1)S(1)} %collective-permute-done.6.x_b, bf16[512,4096]{1,0:T(8,128)(2,1)S(1)} %copy-done, bf16[512,4096]{1,0:T(8,128)(2,1)} %collective-permute-done.3.w_b), custom_call_target="tpu_custom_call" | custom-call | flops 1073741824 | bytes 10485760 | tf_op jit(solution)/shard_map/pallas_call | solution.py:346
  131.1 6.1 %collective-permute-done.9 = bf16[64,4096]{1,0:T(8,128)(2,1)S(1)} collective-permute-done((bf16[64,4096]{1,0:T(8,128)(2,1)S(1)}, bf16[64,4096]{1,0:T(8,128)(2,1)S(1)}, u32[]{:S(2)}, u32[]{:S(2)}) %collective-permute-start.9) | collective-permute-done | bytes 524320 | tf_op jit(solution)/shard_map/ppermute | solution.py:367
  137.2 0.9 add_convert_fusion.1
  138.1 2.5 %collective-permute-start.10 = (bf16[64,4096]{1,0:T(8,128)(2,1)}, bf16[64,4096]{1,0:T(8,128)(2,1)S(1)}, u32[]{:S(2)}, u32[]{:S(2)}) collective-permute-start(bf16[64,4096]{1,0:T(8,128)(2,1)} %add_convert_fusion.1), channel_id=1, source_target_pairs={{0,2},{1,3},{2,6},{3,7},{6,4},{7,5},{4,0},{5,1},{8,10},{9,11},{10,... | collective-permute-start | bytes 1572872 | tf_op jit(solution)/shard_map/ppermute | solution.py:376
  140.6 1.0 slice.38
  141.7 0.7 copy.46
  142.4 6.1 %collective-permute-done.7 = bf16[64,4096]{1,0:T(8,128)(2,1)S(1)} collective-permute-done((bf16[64,4096]{1,0:T(8,128)(2,1)S(1)}, bf16[64,4096]{1,0:T(8,128)(2,1)S(1)}, u32[]{:S(2)}, u32[]{:S(2)}) %collective-permute-start.7) | collective-permute-done | bytes 524320 | tf_op jit(solution)/shard_map/ppermute | solution.py:368
  148.5 13.6 %collective-permute-done.10 = bf16[64,4096]{1,0:T(8,128)(2,1)S(1)} collective-permute-done((bf16[64,4096]{1,0:T(8,128)(2,1)}, bf16[64,4096]{1,0:T(8,128)(2,1)S(1)}, u32[]{:S(2)}, u32[]{:S(2)}) %collective-permute-start.10) | collective-permute-done | bytes 524320 | tf_op jit(solution)/shard_map/ppermute | solution.py:376
  162.1 1.1 add_convert_fusion
  (38 shorter events, 0.4 us)
Async XLA Ops:
  0.6 61.2 %collective-permute-start.3 = (bf16[512,4096]{1,0:T(8,128)(2,1)}, bf16[512,4096]{1,0:T(8,128)(2,1)}, u32[]{:S(2)}, u32[]{:S(2)}) collective-permute-start(bf16[512,4096]{1,0:T(8,128)(2,1)} %w_a.3), channel_id=1, source_target_pairs={{0,1},{1,0},{2,3},{3,2},{4,5},{5,4},{6,7},{7,6},{8,9},{9,8},{10,11... | collective-permute-start | bytes 12582920 | tf_op jit(solution)/shard_map/ppermute | solution.py:406
  3.6 35.6 %collective-permute-start = (s32[32,128]{1,0:T(8,128)}, s32[32,128]{1,0:T(8,128)S(1)}, u32[]{:S(2)}, u32[]{:S(2)}) collective-permute-start(s32[32,128]{1,0:T(8,128)} %shard_map.122), channel_id=1, source_target_pairs={{0,32},{8,40},{16,48},{24,56},{32,0},{40,8},{48,16},{56,24},{64,96... | collective-permute-start | bytes 49160 | tf_op jit(solution)/shard_map/ppermute | solution.py:416
  10.8 15.8 %all-to-all-start = ((s32[32,1,128]{2,1,0:T(1,128)}), s32[32,1,128]{2,1,0:T(1,128)S(1)}, u32[]{:S(2)}, u32[]{:S(2)}) async-start(s32[32,1,128]{2,1,0:T(1,128)} %bitcast.52), calls=%async_computation | async-start | bytes 32768 | tf_op jit(solution)/shard_map/all_to_all | solution.py:409
  18.0 43.8 %collective-permute-start.2 = (bf16[512,512]{1,0:T(8,128)(2,1)}, bf16[512,512]{1,0:T(8,128)(2,1)S(1)}, u32[]{:S(2)}, u32[]{:S(2)}) collective-permute-start(bf16[512,512]{1,0:T(8,128)(2,1)} %q_in.1), channel_id=1, source_target_pairs={{0,32},{8,40},{16,48},{24,56},{32,0},{40,8},{48,16},{56,24},{64,96... | collective-permute-start | bytes 1572872 | tf_op jit(solution)/shard_map/ppermute | solution.py:413
  26.6 0.6 copy-start.5
  31.0 8.5 %copy-start.4 = (s32[32,128]{1,0:T(8,128)S(1)}, s32[32,128]{1,0:T(8,128)}, u32[]{:S(2)}) copy-start(s32[32,128]{1,0:T(8,128)} %shard_map.122) | copy-start | bytes 49156
  31.0 15.4 %copy-start.8 = (s32[1,32]{1,0:T(1,128)S(1)}, s32[1,32]{1,0:T(1,128)}, u32[]{:S(2)}) copy-start(s32[1,32]{1,0:T(1,128)} %param.20) | copy-start | bytes 388
  31.0 15.5 %copy-start.1 = (bf16[512,128]{1,0:T(8,128)(2,1)S(1)}, bf16[512,128]{1,0:T(8,128)(2,1)}, u32[]{:S(2)}) copy-start(bf16[512,128]{1,0:T(8,128)(2,1)} %k_ref) | copy-start | bytes 393220
  31.0 15.5 %copy-start.2 = (bf16[512,128]{1,0:T(8,128)(2,1)S(1)}, bf16[512,128]{1,0:T(8,128)(2,1)}, u32[]{:S(2)}) copy-start(bf16[512,128]{1,0:T(8,128)(2,1)} %v_ref) | copy-start | bytes 393220
  31.0 33.8 %all-to-all-start.1 = ((bf16[16,8,64,128]{3,2,1,0:T(8,128)(2,1)}), bf16[16,8,64,128]{3,2,1,0:T(8,128)(2,1)}, u32[]{:S(2)}, u32[]{:S(2)}) async-start(bf16[16,8,64,128]{3,2,1,0:T(8,128)(2,1)} %shard_map.123), calls=%async_computation.1 | async-start | bytes 4194304 | tf_op jit(solution)/shard_map/all_to_all | solution.py:409
  48.0 9.1 %collective-permute-start.1 = (bf16[16,32,128]{2,1,0:T(8,128)(2,1)S(1)}, bf16[16,32,128]{2,1,0:T(8,128)(2,1)S(1)}, u32[]{:S(2)}, u32[]{:S(2)}) collective-permute-start(bf16[16,32,128]{2,1,0:T(8,128)(2,1)S(1)} %bitcast.55), channel_id=1, source_target_pairs={{0,32},{8,40},{16,48},{24,56},{32,0},{40,8},{48,16},{56,24},{64,96... | collective-permute-start | bytes 393224 | tf_op jit(solution)/shard_map/ppermute | solution.py:442
  57.2 0.7 copy-start.6
  61.8 3.0 %copy-start.7 = (bf16[512,512]{1,0:T(8,128)(2,1)}, bf16[512,512]{1,0:T(8,128)(2,1)S(1)}, u32[]{:S(2)}) copy-start(bf16[512,512]{1,0:T(8,128)(2,1)S(1)} %collective-permute-done.2.q_in) | copy-start | bytes 1572868
  64.8 35.6 %all-to-all-start.2 = ((bf16[16,9,64,128]{3,2,1,0:T(8,128)(2,1)}), bf16[16,9,64,128]{3,2,1,0:T(8,128)(2,1)}, u32[]{:S(2)}, u32[]{:S(2)}) async-start(bf16[16,9,64,128]{3,2,1,0:T(8,128)(2,1)} %shard_map.124), calls=%async_computation.2 | async-start | bytes 4718592 | tf_op jit(solution)/shard_map/all_to_all | solution.py:409
  72.8 27.6 %copy-start.3 = (bf16[512,512]{1,0:T(8,128)(2,1)S(1)}, bf16[512,512]{1,0:T(8,128)(2,1)}, u32[]{:S(2)}) copy-start(bf16[512,512]{1,0:T(8,128)(2,1)} %q_in.1) | copy-start | bytes 1572868
  85.1 30.6 %collective-permute-start.4 = (bf16[512,512]{1,0:T(8,128)(2,1)}, bf16[512,512]{1,0:T(8,128)(2,1)S(1)}, u32[]{:S(2)}, u32[]{:S(2)}) collective-permute-start(bf16[512,512]{1,0:T(8,128)(2,1)} %get-tuple-element.31), channel_id=1, source_target_pairs={{0,32},{8,40},{16,48},{24,56},{32,0},{40,8},{48,16},{56,24},{64,96... | collective-permute-start | bytes 1572872 | tf_op jit(solution)/shard_map/ppermute | solution.py:455
  89.5 26.1 %collective-permute-start.5 = (f32[8,512]{1,0:T(8,128)}, f32[8,512]{1,0:T(8,128)S(1)}, u32[]{:S(2)}, u32[]{:S(2)}) collective-permute-start(f32[8,512]{1,0:T(8,128)} %get-tuple-element.32), channel_id=1, source_target_pairs={{0,32},{8,40},{16,48},{24,56},{32,0},{40,8},{48,16},{56,24},{64,96... | collective-permute-start | bytes 49160 | tf_op jit(solution)/shard_map/ppermute | solution.py:455
  100.4 18.4 %copy-start = (bf16[512,4096]{1,0:T(8,128)(2,1)S(1)}, bf16[512,4096]{1,0:T(8,128)(2,1)}, u32[]{:S(2)}) copy-start(bf16[512,4096]{1,0:T(8,128)(2,1)} %w_a.3) | copy-start | bytes 12582916
  117.1 1.6 collective-permute-start.6
  122.1 15.1 %collective-permute-start.9 = (bf16[64,4096]{1,0:T(8,128)(2,1)S(1)}, bf16[64,4096]{1,0:T(8,128)(2,1)S(1)}, u32[]{:S(2)}, u32[]{:S(2)}) collective-permute-start(bf16[64,4096]{1,0:T(8,128)(2,1)S(1)} %get-tuple-element.42), channel_id=1, source_target_pairs={{0,2},{1,3},{6,4},{7,5},{8,10},{9,11},{14,12},{15,13},{16,18},{17,... | collective-permute-start | bytes 1572872 | tf_op jit(solution)/shard_map/ppermute | solution.py:367
  125.0 23.5 %collective-permute-start.8 = (bf16[64,4096]{1,0:T(8,128)(2,1)S(1)}, bf16[64,4096]{1,0:T(8,128)(2,1)S(1)}, u32[]{:S(2)}, u32[]{:S(2)}) collective-permute-start(bf16[64,4096]{1,0:T(8,128)(2,1)S(1)} %get-tuple-element.42), channel_id=1, source_target_pairs={{2,4},{3,5},{4,2},{5,3},{10,12},{11,13},{12,10},{13,11},{18,20},{1... | collective-permute-start | bytes 1572872 | tf_op jit(solution)/shard_map/ppermute | solution.py:369
  125.7 22.8 %collective-permute-start.7 = (bf16[64,4096]{1,0:T(8,128)(2,1)S(1)}, bf16[64,4096]{1,0:T(8,128)(2,1)S(1)}, u32[]{:S(2)}, u32[]{:S(2)}) collective-permute-start(bf16[64,4096]{1,0:T(8,128)(2,1)S(1)} %get-tuple-element.41), channel_id=1, source_target_pairs={{0,4},{1,5},{6,2},{7,3},{2,0},{3,1},{4,6},{5,7},{8,12},{9,13},{14,... | collective-permute-start | bytes 1572872 | tf_op jit(solution)/shard_map/ppermute | solution.py:368
  138.1 24.0 %collective-permute-start.10 = (bf16[64,4096]{1,0:T(8,128)(2,1)}, bf16[64,4096]{1,0:T(8,128)(2,1)S(1)}, u32[]{:S(2)}, u32[]{:S(2)}) collective-permute-start(bf16[64,4096]{1,0:T(8,128)(2,1)} %add_convert_fusion.1), channel_id=1, source_target_pairs={{0,2},{1,3},{2,6},{3,7},{6,4},{7,5},{4,0},{5,1},{8,10},{9,11},{10,... | collective-permute-start | bytes 1572872 | tf_op jit(solution)/shard_map/ppermute | solution.py:376
